TPU v7x, 256 devices: a whole 4x4x8 slice. The times are simulated.
256 devices in a mesh: grp: 8 (over y, core), dev: 32 (over x, z).
Axes of the slice: x: 4, y: 4, z: 8, core: 2. Of those that a mesh axis runs over, the one named last changes fastest.
Arguments:
- strengths: bfloat16 [131072, 256], P(('grp', 'dev')), may hold values from 0.099609375 to 1
- source_counts: int32 [131072], P(('grp', 'dev')), may hold values from 1 to 256
- source_map: bfloat16 [256, 98], replicated, may hold values from -0.375 to 0.375
- merge_ops: bfloat16 [8, 98, 98], replicated, may hold values from -0.21875 to 0.21875
- translate_ops: bfloat16 [189, 98, 98], replicated, may hold values from -0.046875 to 0.046875
- spread_ops: bfloat16 [8, 98, 98], replicated, may hold values from -0.625 to 0.625
- leaf_lists: int32 [189, 131072], P(None, ('grp', 'dev')), may hold values from -1 to 1023, as said below
- parent_lists: int32 [189, 16384], P(None, ('grp', 'dev')), may hold values from -1 to 127, as said below
- grand_lists: int32 [189, 2048], P(None, ('grp', 'dev')), may hold values from -1 to 15, as said below
- top_lists: int32 [189, 256], P(None, ('grp', 'dev')), may hold values from -1 to 255, as said below
Outputs:
- leaf_local: float32 [98, 131072], P(None, ('grp', 'dev'))
Inputs may be any that keep to these rules, and one draw needn't show every extreme that they name: `leaf_lists`: each entry is -1 or names an existing leaf box; both ends of the range are reached in every draw. `parent_lists`: each entry is -1 or names an existing box of that level; both ends are reached. `grand_lists`: each entry is -1 or names an existing box of that level; both ends are reached. `top_lists`: each entry is -1 or any box of that level.
All inputs are finite; a program needn't handle non-finite values.
Results may differ from a plain program's by a relative error of at most 0.0055.
Values may be sent and summed in bfloat16 or wider, within the bound.
A program may use at most 128 MiB of HBM per device.

v0:
```python
import jax
import jax.numpy as jnp
from jax import lax
from jax.sharding import PartitionSpec as P


def from_behind(block, axis, distance):
    devices = range(lax.axis_size(axis))
    route = [(i - distance, i) for i in devices if i - distance in devices]
    return lax.ppermute(block, axis, route)


def sources_up(strengths, source_counts, source_map):
    slot_ids = jnp.arange(strengths.shape[1], dtype=jnp.int32)
    is_live = slot_ids[None, :] < source_counts[:, None]
    masked = jnp.where(is_live, strengths, jnp.zeros_like(strengths))
    return lax.dot_general(
        source_map, masked, (((0,), (1,)), ((), ())), preferred_element_type=jnp.float32
    ).astype(jnp.bfloat16)


def merge_children(child_m, merge_ops):
    grouped = child_m.reshape(child_m.shape[0], child_m.shape[1] // 8, 8)
    return jnp.einsum("cqp,pjc->qj", merge_ops, grouped, preferred_element_type=jnp.float32).astype(
        jnp.bfloat16
    )


def spread_children(parent_local, spread_ops):
    rounded = parent_local.astype(jnp.bfloat16)
    children = jnp.einsum("cqp,pj->qjc", spread_ops, rounded, preferred_element_type=jnp.float32)
    return children.reshape(children.shape[0], -1)


def translate_window(window, table_rows, operators, anchor, factor):
    kcount = table_rows.shape[0]
    block_size = -(-kcount // 4)
    width = window.shape[1]
    padded = jnp.concatenate([window, jnp.zeros((window.shape[0], 1), window.dtype)], axis=1)
    summed = jnp.zeros((window.shape[0], table_rows.shape[1]), jnp.float32)
    for first_class in range(0, kcount, block_size):
        class_rows = table_rows[first_class : first_class + block_size]
        offset = jnp.where(class_rows >= 0, jnp.clip(class_rows - anchor, 0, width - 1), width)
        picked = jnp.take(padded, offset, axis=1)
        summed = summed + jnp.einsum(
            "kqp,pkn->qn",
            operators[first_class : first_class + block_size],
            picked,
            preferred_element_type=jnp.float32,
        )
    return factor * summed


def per_device(
    strengths,
    source_counts,
    source_map,
    merge_ops,
    translate_ops,
    spread_ops,
    leaf_lists,
    parent_lists,
    grand_lists,
    top_lists,
):
    leaf_m = sources_up(strengths, source_counts, source_map)
    leaf_count = leaf_m.shape[1]
    parent_m = merge_children(leaf_m, merge_ops)
    grand_m = merge_children(parent_m, merge_ops)
    top_m = merge_children(grand_m, merge_ops)
    position = lax.axis_index(("grp", "dev"))
    parent_count = parent_m.shape[1]
    grand_count = grand_m.shape[1]
    from_below = from_behind(
        (
            leaf_m[:, leaf_count // 2 :],
            parent_m[:, parent_count // 2 :],
            grand_m[:, grand_count // 2 :],
        ),
        ("grp", "dev"),
        1,
    )
    from_above = from_behind(
        (
            leaf_m[:, : leaf_count // 2],
            parent_m[:, : parent_count // 2],
            grand_m[:, : grand_count // 2],
        ),
        ("grp", "dev"),
        -1,
    )
    owned = (leaf_m, parent_m, grand_m)
    counts_level = (leaf_count, parent_count, grand_count)
    windows = [
        jnp.concatenate([from_below[level], owned[level], from_above[level]], axis=1)
        for level in range(3)
    ]
    anchors = [position * counts_level[level] - counts_level[level] // 2 for level in range(3)]
    relatives = (leaf_lists, parent_lists, grand_lists)
    absolutes = [
        jnp.where(relatives[level] >= 0, relatives[level] + anchors[level], -1)
        for level in range(3)
    ]
    piece_rows = lax.all_gather(top_m, ("grp", "dev"), axis=1, tiled=True)
    is_valid = (top_lists >= 0) & (top_lists >= 0) & (top_lists < piece_rows.shape[1])
    picked = jnp.take(piece_rows, jnp.clip(top_lists, 0, piece_rows.shape[1] - 1), axis=1)
    gathered = jnp.where(is_valid[None], picked, jnp.zeros_like(picked)).astype(jnp.float32)
    top_local = 0.125 * jnp.einsum(
        "kqp,pkn->qn",
        translate_ops,
        gathered.astype(jnp.bfloat16),
        preferred_element_type=jnp.float32,
    )
    grand_local = translate_window(
        windows[2], absolutes[2], translate_ops, anchors[2], 0.25
    ) + spread_children(top_local, spread_ops)
    parent_local = translate_window(
        windows[1], absolutes[1], translate_ops, anchors[1], 0.5
    ) + spread_children(grand_local, spread_ops)
    return translate_window(
        windows[0], absolutes[0], translate_ops, anchors[0], 1.0
    ) + spread_children(parent_local, spread_ops)


def solution(mesh):
    return jax.shard_map(
        per_device,
        mesh=mesh,
        in_specs=(
            P(("grp", "dev"), None),
            P(("grp", "dev")),
            P(),
            P(),
            P(),
            P(),
            P(None, ("grp", "dev")),
            P(None, ("grp", "dev")),
            P(None, ("grp", "dev")),
            P(None, ("grp", "dev")),
        ),
        out_specs=P(None, ("grp", "dev")),
        check_vma=False,
    )
```

profile of v0, /device:TPU:1, one launch (start us, length us, event | category | flops | bytes accessed | tf_op | source)
XLA Modules:
  0.0 522.8 jit_solution(7886014880221073787)
XLA Ops:
  0.0 1.3 fusion.49
  1.5 1.1 copy.206
  3.0 0.6 fusion.178
  3.7 4.4 collective-permute-start.4
  8.0 8.6 %collective-permute-start.5 = (bf16[98,4]{0,1:T(4,128)(2,1)}, bf16[98,4]{0,1:T(4,128)(2,1)}, u32[]{:S(2)}, u32[]{:S(2)}) collective-permute-start(bf16[98,4]{0,1:T(4,128)(2,1)} %get-tuple-element.50), channel_id=1, source_target_pairs={{1,0},{2,1},{3,2},{4,3},{5,4},{6,5},{7,6},{8,7},{9,8},{10,9},{11,1... | collective-permute-start | bytes 2360 | tf_op jit(solution)/shard_map/ppermute | solution.py:10
  17.2 1.9 collective-permute-start.2
  19.2 7.0 %collective-permute-start.3 = (bf16[98,32]{0,1:T(8,128)(2,1)}, bf16[98,32]{0,1:T(8,128)(2,1)}, u32[]{:S(2)}, u32[]{:S(2)}) collective-permute-start(bf16[98,32]{0,1:T(8,128)(2,1)} %get-tuple-element.44), channel_id=1, source_target_pairs={{1,0},{2,1},{3,2},{4,3},{5,4},{6,5},{7,6},{8,7},{9,8},{10,9},{11,1... | collective-permute-start | bytes 18824 | tf_op jit(solution)/shard_map/ppermute | solution.py:10
  26.1 0.6 fusion.176
  26.8 1.9 collective-permute-start
  29.3 0.7 compare_and_fusion.11
  30.0 3.7 fusion.175
  33.7 3.3 slice.83
  37.0 0.7 compare_and_fusion.6
  37.7 0.7 compare_and_fusion.7
  38.4 1.0 add_select_fusion
  39.6 0.8 compare_and_fusion
  40.4 0.7 compare_and_fusion.3
  41.8 0.7 copy.194
  43.3 0.7 copy.192
  45.7 54.0 %all-gather = bf16[256,1,98]{2,1,0:T(2,128)(2,1)S(1)} all-gather(bf16[1,1,98]{2,1,0:T(2,128)(2,1)S(1)} %fusion.72), channel_id=1, replica_groups=mesh['grp'=8,'dev'=32] {'grp','dev'}, dimensions={0}, use_global_device_ids=true | all-gather | bytes 50372 | tf_op jit(solution)/shard_map/all_gather | solution.py:104
  99.7 0.7 and_reduce_fusion
  100.4 0.8 copy.185
  101.3 0.6 broadcast_clamp_fusion.3
  102.1 0.6 broadcast_clamp_fusion.4
  102.7 0.8 copy.187
  103.6 0.6 pad_clamp_fusion.1
  105.0 0.7 broadcast_clamp_fusion.2
  105.7 0.6 broadcast_clamp_fusion.1
  106.4 0.6 broadcast_clamp_fusion
  107.0 0.8 gather_fusion.3
  108.0 5.3 %fusion.83 = f32[1,8,98]{2,0,1:T(1,128)S(1)} fusion(bf16[189,98,98]{2,0,1:T(8,128)(2,1)} %param.20, bf16[8,98,98]{2,0,1:T(8,128)(2,1)S(1)} %copy-done, bf16[98,189,1]{0,1,2:T(8,128)(2,1)S(1)} %select_bitcast_fusion), kind=kOutput, calls=%fused_computation.83 | convolution fusion | flops 3784172 | bytes 3824156 | tf_op jit(solution)/shard_map/cqp,pj->qjc/dot_general | solution.py:31
  113.6 0.7 copy.184
  114.3 0.7 copy.182
  115.0 0.7 copy.186
  115.7 0.7 copy.177
  116.9 6.1 %collective-permute-start.1 = (bf16[98,256]{1,0:T(8,128)(2,1)}, bf16[98,256]{1,0:T(8,128)(2,1)}, u32[]{:S(2)}, u32[]{:S(2)}) collective-permute-start(bf16[98,256]{1,0:T(8,128)(2,1)} %get-tuple-element.38), channel_id=1, source_target_pairs={{1,0},{2,1},{3,2},{4,3},{5,4},{6,5},{7,6},{8,7},{9,8},{10,9},{11,1... | collective-permute-start | bytes 150536 | tf_op jit(solution)/shard_map/ppermute | solution.py:10
  123.1 0.7 pad_maximum_fusion.1
  123.8 1.4 gather_fusion.12
  125.3 1.4 gather_fusion.11
  126.7 1.4 gather_fusion.2
  128.2 1.4 gather_fusion.10
  131.7 1.3 convolution_bitcast_fusion.1
  133.0 0.7 pad_maximum_fusion
  133.8 9.2 %gather_fusion.9 = bf16[3072,98]{1,0:T(8,128)(2,1)S(1)} fusion(bf16[98,129]{0,1:T(8,128)(2,1)S(1)} %pad_maximum_fusion, s32[3072]{0:T(1024)S(1)} %copy-done.18), kind=kCustom, calls=%fused_computation.6.clone | custom fusion | bytes 1216512 | tf_op jit(solution)/shard_map/jit(_take)/gather | solution.py:44
  142.9 9.2 %gather_fusion.8 = bf16[3072,98]{1,0:T(8,128)(2,1)S(1)} fusion(bf16[98,129]{0,1:T(8,128)(2,1)S(1)} %pad_maximum_fusion, s32[3072]{0:T(1024)S(1)} %copy-done.19), kind=kCustom, calls=%fused_computation.5.clone | custom fusion | bytes 1216512 | tf_op jit(solution)/shard_map/jit(_take)/gather | solution.py:44
  152.1 6.1 %gather_fusion.1 = bf16[2880,98]{1,0:T(8,128)(2,1)S(1)} fusion(bf16[98,129]{0,1:T(8,128)(2,1)S(1)} %pad_maximum_fusion, s32[3072]{0:T(1024)S(1)} %copy-done.20), kind=kCustom, calls=%fused_computation.10 | custom fusion | bytes 1140480 | tf_op jit(solution)/shard_map/jit(_take)/gather | solution.py:44
  158.3 9.2 %gather_fusion.7 = bf16[3072,98]{1,0:T(8,128)(2,1)S(1)} fusion(bf16[98,129]{0,1:T(8,128)(2,1)S(1)} %pad_maximum_fusion, s32[3072]{0:T(1024)S(1)} %copy-done.21), kind=kCustom, calls=%fused_computation.1.clone | custom fusion | bytes 1216512 | tf_op jit(solution)/shard_map/jit(_take)/gather | solution.py:44
  167.5 2.9 convolution_bitcast_fusion.3
  171.0 0.7 copy-done.9
  172.3 0.7 copy-done.7
  173.0 0.8 convolution_bitcast_fusion
  174.1 0.9 maximum_maximum_fusion
  175.2 85.9 %gather_fusion.4 = bf16[24576,98]{1,0:T(8,128)(2,1)} fusion(bf16[98,1025]{0,1:T(8,128)(2,1)S(1)} %copy.165, s32[24576]{0:T(1024)S(1)} %copy-done.11), kind=kCustom, calls=%fused_computation.clone | custom fusion | bytes 9732096 | tf_op jit(solution)/shard_map/jit(_take)/gather | solution.py:44
  261.0 8.5 %copy.166 = bf16[48,512,98]{1,2,0:T(8,128)(2,1)} copy(bf16[48,512,98]{2,1,0:T(8,128)(2,1)} %bitcast.271) | data formatting | bytes 9633792 | tf_op jit(solution)/shard_map/jit(_take)/gather | solution.py:44
  269.5 85.9 %gather_fusion.5 = bf16[24576,98]{1,0:T(8,128)(2,1)} fusion(bf16[98,1025]{0,1:T(8,128)(2,1)S(1)} %copy.165, s32[24576]{0:T(1024)S(1)} %copy-done.12), kind=kCustom, calls=%fused_computation.3.clone | custom fusion | bytes 9732096 | tf_op jit(solution)/shard_map/jit(_take)/gather | solution.py:44
  355.4 8.4 %copy.169 = bf16[48,512,98]{1,2,0:T(8,128)(2,1)} copy(bf16[48,512,98]{2,1,0:T(8,128)(2,1)} %bitcast.272) | data formatting | bytes 9633792 | tf_op jit(solution)/shard_map/jit(_take)/gather | solution.py:44
  363.8 85.9 %gather_fusion.6 = bf16[24576,98]{1,0:T(8,128)(2,1)} fusion(bf16[98,1025]{0,1:T(8,128)(2,1)S(1)} %copy.165, s32[24576]{0:T(1024)S(1)} %copy-done.13), kind=kCustom, calls=%fused_computation.4.clone | custom fusion | bytes 9732096 | tf_op jit(solution)/shard_map/jit(_take)/gather | solution.py:44
  449.7 8.4 %copy.172 = bf16[48,512,98]{1,2,0:T(8,128)(2,1)} copy(bf16[48,512,98]{2,1,0:T(8,128)(2,1)} %bitcast.273) | data formatting | bytes 9633792 | tf_op jit(solution)/shard_map/jit(_take)/gather | solution.py:44
  458.1 46.6 %gather_fusion = bf16[23040,98]{1,0:T(8,128)(2,1)} fusion(bf16[98,1025]{0,1:T(8,128)(2,1)S(1)} %copy.165, s32[23552]{0:T(1024)S(1)} %pad_clamp_fusion), kind=kCustom, calls=%fused_computation.9 | custom fusion | bytes 9123840 | tf_op jit(solution)/shard_map/jit(_take)/gather | solution.py:44
  504.7 8.4 %copy.175 = bf16[45,512,98]{1,2,0:T(8,128)(2,1)} copy(bf16[45,512,98]{2,1,0:T(8,128)(2,1)} %bitcast.274) | data formatting | bytes 9031680 | tf_op jit(solution)/shard_map/jit(_take)/gather | solution.py:44
  513.1 3.8 fusion.25
  517.2 1.2 fusion.46
  519.2 1.2 fusion.43
  520.9 1.9 fusion.40
  (153 shorter events, 12.6 us)
Async XLA Ops:
  0.0 107.9 %copy-start = (bf16[8,98,98]{2,0,1:T(8,128)(2,1)S(1)}, bf16[8,98,98]{2,0,1:T(8,128)(2,1)}, u32[]{:S(2)}) copy-start(bf16[8,98,98]{2,0,1:T(8,128)(2,1)} %param.21) | copy-start | bytes 460996
  0.0 28.7 %copy-start.32 = (s32[189,8]{0,1:T(8,128)S(1)}, s32[189,8]{0,1:T(8,128)}, u32[]{:S(2)}) copy-start(s32[189,8]{0,1:T(8,128)} %param.24) | copy-start | bytes 18148
  3.7 113.3 %collective-permute-start.4 = (bf16[98,4]{0,1:T(4,128)(2,1)}, bf16[98,4]{0,1:T(4,128)(2,1)}, u32[]{:S(2)}, u32[]{:S(2)}) collective-permute-start(bf16[98,4]{0,1:T(4,128)(2,1)} %get-tuple-element.49), channel_id=1, source_target_pairs={{0,1},{1,2},{2,3},{3,4},{4,5},{5,6},{6,7},{7,8},{8,9},{9,10},{10,1... | collective-permute-start | bytes 2360 | tf_op jit(solution)/shard_map/ppermute | solution.py:10
  8.0 115.0 %collective-permute-start.5 = (bf16[98,4]{0,1:T(4,128)(2,1)}, bf16[98,4]{0,1:T(4,128)(2,1)}, u32[]{:S(2)}, u32[]{:S(2)}) collective-permute-start(bf16[98,4]{0,1:T(4,128)(2,1)} %get-tuple-element.50), channel_id=1, source_target_pairs={{1,0},{2,1},{3,2},{4,3},{5,4},{6,5},{7,6},{8,7},{9,8},{10,9},{11,1... | collective-permute-start | bytes 2360 | tf_op jit(solution)/shard_map/ppermute | solution.py:10
  17.2 115.8 %collective-permute-start.2 = (bf16[98,32]{0,1:T(8,128)(2,1)}, bf16[98,32]{0,1:T(8,128)(2,1)}, u32[]{:S(2)}, u32[]{:S(2)}) collective-permute-start(bf16[98,32]{0,1:T(8,128)(2,1)} %get-tuple-element.43), channel_id=1, source_target_pairs={{0,1},{1,2},{2,3},{3,4},{4,5},{5,6},{6,7},{7,8},{8,9},{9,10},{10,1... | collective-permute-start | bytes 18824 | tf_op jit(solution)/shard_map/ppermute | solution.py:10
  19.2 113.8 %collective-permute-start.3 = (bf16[98,32]{0,1:T(8,128)(2,1)}, bf16[98,32]{0,1:T(8,128)(2,1)}, u32[]{:S(2)}, u32[]{:S(2)}) collective-permute-start(bf16[98,32]{0,1:T(8,128)(2,1)} %get-tuple-element.44), channel_id=1, source_target_pairs={{1,0},{2,1},{3,2},{4,3},{5,4},{6,5},{7,6},{8,7},{9,8},{10,9},{11,1... | collective-permute-start | bytes 18824 | tf_op jit(solution)/shard_map/ppermute | solution.py:10
  26.8 147.3 %collective-permute-start = (bf16[98,256]{1,0:T(8,128)(2,1)}, bf16[98,256]{1,0:T(8,128)(2,1)}, u32[]{:S(2)}, u32[]{:S(2)}) collective-permute-start(bf16[98,256]{1,0:T(8,128)(2,1)} %get-tuple-element.37), channel_id=1, source_target_pairs={{0,1},{1,2},{2,3},{3,4},{4,5},{5,6},{6,7},{7,8},{8,9},{9,10},{10,1... | collective-permute-start | bytes 150536 | tf_op jit(solution)/shard_map/ppermute | solution.py:10
  33.7 96.0 %copy-start.1 = (bf16[48,98,98]{2,0,1:T(8,128)(2,1)}, bf16[48,98,98]{2,0,1:T(8,128)(2,1)S(1)}, u32[]{:S(2)}) copy-start(bf16[48,98,98]{2,0,1:T(8,128)(2,1)S(1)} %get-tuple-element.29) | copy-start | bytes 2765956
  33.7 96.5 %copy-start.3 = (bf16[48,98,98]{2,0,1:T(8,128)(2,1)}, bf16[48,98,98]{2,0,1:T(8,128)(2,1)S(1)}, u32[]{:S(2)}) copy-start(bf16[48,98,98]{2,0,1:T(8,128)(2,1)S(1)} %get-tuple-element.30) | copy-start | bytes 2765956
  33.7 3.3 copy-start.22
  108.0 5.4 %copy-start.40 = (pred[45,8]{0,1:T(8,128)(4,1)S(1)}, pred[45,8]{0,1:T(8,128)(4,1)}, u32[]{:S(2)}) copy-start(pred[45,8]{0,1:T(8,128)(4,1)} %get-tuple-element.16) | copy-start | bytes 1084
  108.0 5.5 %copy-start.39 = (pred[48,8]{0,1:T(8,128)(4,1)S(1)}, pred[48,8]{0,1:T(8,128)(4,1)}, u32[]{:S(2)}) copy-start(pred[48,8]{0,1:T(8,128)(4,1)} %get-tuple-element.10) | copy-start | bytes 1156
  108.0 5.6 %copy-start.25 = (pred[48,64]{0,1:T(8,128)(4,1)S(1)}, pred[48,64]{0,1:T(8,128)(4,1)}, u32[]{:S(2)}) copy-start(pred[48,64]{0,1:T(8,128)(4,1)} %get-tuple-element.41) | copy-start | bytes 9220
  108.0 6.3 %copy-start.24 = (pred[48,64]{0,1:T(8,128)(4,1)S(1)}, pred[48,64]{0,1:T(8,128)(4,1)}, u32[]{:S(2)}) copy-start(pred[48,64]{0,1:T(8,128)(4,1)} %get-tuple-element.39) | copy-start | bytes 9220
  108.0 7.0 %copy-start.26 = (pred[45,64]{0,1:T(8,128)(4,1)S(1)}, pred[45,64]{0,1:T(8,128)(4,1)}, u32[]{:S(2)}) copy-start(pred[45,64]{0,1:T(8,128)(4,1)} %get-tuple-element.26) | copy-start | bytes 8644
  108.0 7.7 %copy-start.23 = (pred[48,64]{0,1:T(8,128)(4,1)S(1)}, pred[48,64]{0,1:T(8,128)(4,1)}, u32[]{:S(2)}) copy-start(pred[48,64]{0,1:T(8,128)(4,1)} %get-tuple-element.20) | copy-start | bytes 9220
  108.0 15.8 %copy-start.14 = (s32[1024]{0:T(1024)S(1)}, s32[1024]{0:T(1024)}, u32[]{:S(2)}) copy-start(s32[1024]{0:T(1024)} %pad_clamp_fusion.4) | copy-start | bytes 12292
  116.9 57.1 %collective-permute-start.1 = (bf16[98,256]{1,0:T(8,128)(2,1)}, bf16[98,256]{1,0:T(8,128)(2,1)}, u32[]{:S(2)}, u32[]{:S(2)}) collective-permute-start(bf16[98,256]{1,0:T(8,128)(2,1)} %get-tuple-element.38), channel_id=1, source_target_pairs={{1,0},{2,1},{3,2},{4,3},{5,4},{6,5},{7,6},{8,7},{9,8},{10,9},{11,1... | collective-permute-start | bytes 150536 | tf_op jit(solution)/shard_map/ppermute | solution.py:10
  123.8 1.5 copy-start.15
  125.3 1.5 copy-start.16
  126.7 1.5 copy-start.17
  128.2 1.5 copy-start.37
  129.7 0.7 copy-start.38
  129.7 1.3 copy-start.8
  130.4 1.4 copy-start.6
  131.0 2.8 copy-start.18
  133.7 9.2 %copy-start.19 = (s32[3072]{0:T(1024)S(1)}, s32[3072]{0:T(1024)}, u32[]{:S(2)}) copy-start(s32[3072]{0:T(1024)} %broadcast_clamp_fusion.4) | copy-start | bytes 36868
  142.9 9.2 %copy-start.20 = (s32[3072]{0:T(1024)S(1)}, s32[3072]{0:T(1024)}, u32[]{:S(2)}) copy-start(s32[3072]{0:T(1024)} %pad_clamp_fusion.1) | copy-start | bytes 36868
  152.1 6.2 %copy-start.21 = (s32[3072]{0:T(1024)S(1)}, s32[3072]{0:T(1024)}, u32[]{:S(2)}) copy-start(s32[3072]{0:T(1024)} %broadcast_clamp_fusion.5) | copy-start | bytes 36868
  158.3 9.2 %copy-start.36 = (pred[48,64]{1,0:T(8,128)(4,1)S(1)}, pred[48,64]{1,0:T(8,128)(4,1)}, u32[]{:S(2)}) copy-start(pred[48,64]{1,0:T(8,128)(4,1)} %copy.184) | copy-start | bytes 9220
  167.5 2.9 copy-start.4
  167.5 2.9 copy-start.33
  170.4 1.3 copy-start.9
  170.4 1.3 copy-start.34
  171.7 1.3 copy-start.7
  171.7 1.3 copy-start.35
  171.7 1.3 copy-start.41
  171.7 1.3 copy-start.42
  173.0 1.1 copy-start.31
  173.7 1.4 copy-start.11
  261.0 8.5 %copy-start.12 = (s32[24576]{0:T(1024)S(1)}, s32[24576]{0:T(1024)}, u32[]{:S(2)}) copy-start(s32[24576]{0:T(1024)} %broadcast_clamp_fusion.1) | copy-start | bytes 294916
  355.4 8.4 %copy-start.13 = (s32[24576]{0:T(1024)S(1)}, s32[24576]{0:T(1024)}, u32[]{:S(2)}) copy-start(s32[24576]{0:T(1024)} %broadcast_clamp_fusion) | copy-start | bytes 294916
  504.7 8.4 %copy-start.30 = (pred[48,512]{1,0:T(8,128)(4,1)S(1)}, pred[48,512]{1,0:T(8,128)(4,1)}, u32[]{:S(2)}) copy-start(pred[48,512]{1,0:T(8,128)(4,1)} %get-tuple-element.33) | copy-start | bytes 73732
  504.7 12.2 %slice-start.2 = ((s8[5111808]{0:T(1024)(128)(4,1)}), s8[917504]{0:T(1024)(128)(4,1)S(1)}, s32[]{:S(2)}) async-start(s8[5111808]{0:T(1024)(128)(4,1)} %bitcast.277), calls=%async_computation.2 | async-start | bytes 1835008
  513.1 3.9 slice-start.3
  513.1 4.1 copy-start.5
  513.1 4.1 copy-start.29
  513.1 5.3 %slice-start = ((s8[5111808]{0:T(1024)(128)(4,1)}), s8[4194304]{0:T(1024)(128)(4,1)S(1)}, s32[]{:S(2)}) async-start(s8[5111808]{0:T(1024)(128)(4,1)} %bitcast.275), calls=%async_computation | async-start | bytes 8388608
  517.1 1.7 slice-start.1
  517.2 2.0 copy-start.2
  517.2 2.0 copy-start.28
  517.2 3.3 slice-start.4
  519.2 1.3 slice-start.5
  519.2 1.7 copy-start.10
  519.2 1.7 copy-start.27
where the time goes:
time: 524 us; the launch traced here: 523 us
  local copies, waits for them, and re-layouts  400 us (76%)
  blocking collectives  54 us (10%)
  starting transfers between devices  29.9 us (6%)
  matrix products  22.8 us (4%)
  other arithmetic  15.2 us (3%)
    gather x16, local copies, waits for them, and re-layouts, translate_window(): picked = jnp.take(padded, offset, axis=1)  377 us
    all_gather x1, blocking collectives, per_device(): piece_rows = lax.all_gather(top_m, ('grp', 'dev'), axis=1, tiled=True)  54 us
    ppermute x6, starting transfers between devices, from_behind(): return lax.ppermute(block, axis, route)  29.9 us
    dot_general x10, matrix products, translate_window(): jnp.einsum('kqp,pkn->qn', operators[first_class:first_class + block_size]...  13.5 us
  transfers between devices with their start and end apart: 6, of which 0 were waited for; matrix products, arithmetic and copies ran while one was open for 16% of the time, Pallas kernels for 0%

commit v1 on v0

v1 whole, which is shorter than its diff:
```python
import jax
import jax.numpy as jnp
from jax import lax
from jax.experimental import pallas as pl
from jax.experimental.pallas import tpu as pltpu
from jax.sharding import PartitionSpec as P

BF = jnp.bfloat16
F32 = jnp.float32
ROWS = 104
MESH = pl.DeviceIdType.MESH
NT = (((1,), (1,)), ((), ()))


def up_kernel(
    grps, devs, strengths, counts, smap, mg, leaf_out, mid_out, top_out,
    m_ref, leaf_t, par_t, gra_t, mine, got, midm, midg, msg, buf_a, msg_b, buf_b,
    send_l, recv_l, send_m, recv_m, send_a, recv_a, send_b, recv_b,
):
    g = lax.axis_index("grp")
    d = lax.axis_index("dev")
    total = grps * devs
    me = g * devs + d
    above = lax.rem(me + 1, total)
    below = lax.rem(me + total - 1, total)

    def at(pos):
        return (pos // devs, lax.rem(pos, devs))

    barrier = pltpu.get_barrier_semaphore()

    def greet(pos):
        pl.semaphore_signal(barrier, inc=1, device_id=pos, device_id_type=MESH)

    greet(at(above))
    greet(at(below))
    lax.fori_loop(1, grps, lambda i, c: (greet((lax.rem(g + i, grps), d)), c)[1], 0)
    lax.fori_loop(1, devs, lambda i, c: (greet((g, lax.rem(d + i, devs))), c)[1], 0)

    cnt = jnp.concatenate(
        [jnp.broadcast_to(counts[:, 128 * i : 128 * i + 128], (128, 128)).T for i in range(4)], axis=0
    ).astype(jnp.int16)
    slot = lax.broadcasted_iota(jnp.int16, (512, 128), 1)
    zero = jnp.zeros((512, 128), BF)
    live = jnp.concatenate(
        [
            jnp.where(slot < cnt, strengths[:, 0:128], zero),
            jnp.where(slot + jnp.int16(128) < cnt, strengths[:, 128:256], zero),
        ],
        axis=1,
    )
    leaf_t[...] = jnp.zeros_like(leaf_t)
    par_t[...] = jnp.zeros_like(par_t)
    gra_t[...] = jnp.zeros_like(gra_t)
    m_ref[...] = jnp.zeros_like(m_ref)
    lt = lax.dot_general(live, smap[...], NT, preferred_element_type=F32)
    leaf_t[:, 0:98] = lt.astype(BF).astype(F32)
    for half in range(2):
        mine[half] = jnp.concatenate(
            [leaf_t[256 * half + 128 * i : 256 * half + 128 * i + 128, :].T[0:112] for i in range(2)], axis=1
        ).astype(BF)

    def copy(src, dst, ss, rs, pos):
        return pltpu.make_async_remote_copy(
            src_ref=src, dst_ref=dst, send_sem=ss, recv_sem=rs, device_id=pos, device_id_type=MESH
        )

    pl.semaphore_wait(barrier, 2 + grps - 1 + devs - 1)
    leaf_up = copy(mine.at[1], got.at[0], send_l.at[0], recv_l.at[0], at(above))
    leaf_dn = copy(mine.at[0], got.at[1], send_l.at[1], recv_l.at[1], at(below))
    leaf_up.start()
    leaf_dn.start()

    for q in range(98):
        m_ref[pl.ds(q, 8, stride=ROWS), 0:98] = mg[q].astype(F32)
    merge = jnp.concatenate([m_ref[ROWS * c : ROWS * c + ROWS, :].astype(BF) for c in range(8)], axis=1)

    def merged(kids):
        x = jnp.concatenate([k.astype(BF) for k in kids], axis=1)
        y = lax.dot_general(x, merge, NT, preferred_element_type=F32)
        return y.astype(BF).astype(F32)

    par_t[:, 0:ROWS] = merged([leaf_t[pl.ds(c, 64, stride=8), :] for c in range(8)])
    gra_t[:, 0:ROWS] = merged([par_t[pl.ds(c, 8, stride=8), :] for c in range(8)])
    msg[...] = jnp.zeros_like(msg)
    msg[:, 0:ROWS] = merged([jnp.broadcast_to(gra_t[c : c + 1, :], (8, 128)) for c in range(8)])

    def send_top(i, c):
        to = lax.rem(g + i, grps)
        copy(msg, buf_a.at[g], send_a.at[i], recv_a.at[g], (to, d)).start()
        return c

    lax.fori_loop(1, grps, send_top, 0)

    both = jnp.concatenate([par_t[...], gra_t[...], jnp.zeros((56, 128), F32)], axis=0)
    midm[...] = both.T[0:112].astype(BF)
    mid_up = copy(midm, midg.at[0], send_m.at[0], recv_m.at[0], at(above))
    mid_dn = copy(midm, midg.at[1], send_m.at[1], recv_m.at[1], at(below))
    mid_up.start()
    mid_dn.start()

    sub = lax.broadcasted_iota(jnp.int32, (8, 128), 0)

    def wait_top(i, c):
        frm = lax.rem(g + i, grps)
        w = copy(msg, buf_a.at[frm], send_a.at[i], recv_a.at[frm], (frm, d))
        w.wait_send()
        w.wait_recv()
        return jnp.where(sub == frm, buf_a[frm], c)

    msg_b[...] = lax.fori_loop(1, grps, wait_top, msg[...])

    def send_block(i, c):
        to = lax.rem(d + i, devs)
        copy(msg_b, buf_b.at[d], send_b.at[i], recv_b.at[d], (g, to)).start()
        return c

    lax.fori_loop(1, devs, send_block, 0)
    leaf_up.wait()
    leaf_dn.wait()
    leaf_out[0] = got[0]
    leaf_out[1] = mine[0]
    leaf_out[2] = mine[1]
    leaf_out[3] = got[1]
    mid_up.wait()
    mid_dn.wait()
    mid_out[0] = midg[0]
    mid_out[1] = midm[...]
    mid_out[2] = midg[1]

    def wait_block(i, c):
        frm = lax.rem(d + i, devs)
        w = copy(msg_b, buf_b.at[frm], send_b.at[i], recv_b.at[frm], (g, frm))
        w.wait_send()
        w.wait_recv()
        top_out[frm] = buf_b[frm]
        return c

    top_out[d] = msg_b[...]
    lax.fori_loop(1, devs, wait_block, 0)


def go_up(mesh, strengths, counts, smap, mg):
    grps, devs = mesh.shape["grp"], mesh.shape["dev"]
    vmem = pl.BlockSpec(memory_space=pltpu.VMEM)
    dma = pltpu.SemaphoreType.DMA
    return pl.pallas_call(
        lambda *refs: up_kernel(grps, devs, *refs),
        out_shape=(
            jax.ShapeDtypeStruct((4, 112, 256), BF),
            jax.ShapeDtypeStruct((3, 112, 128), BF),
            jax.ShapeDtypeStruct((devs, grps, 128), F32),
        ),
        in_specs=[vmem] * 4,
        out_specs=(vmem,) * 3,
        scratch_shapes=[
            pltpu.VMEM((8 * ROWS, 128), F32),
            pltpu.VMEM((512, 128), F32),
            pltpu.VMEM((64, 128), F32),
            pltpu.VMEM((8, 128), F32),
            pltpu.VMEM((2, 112, 256), BF),
            pltpu.VMEM((2, 112, 256), BF),
            pltpu.VMEM((112, 128), BF),
            pltpu.VMEM((2, 112, 128), BF),
            pltpu.VMEM((8, 128), F32),
            pltpu.VMEM((grps, 8, 128), F32),
            pltpu.VMEM((8, 128), F32),
            pltpu.VMEM((devs, 8, 128), F32),
            dma((2,)), dma((2,)), dma((2,)), dma((2,)),
            dma((grps,)), dma((grps,)), dma((devs,)), dma((devs,)),
        ],
        compiler_params=pltpu.CompilerParams(
            collective_id=0, has_side_effects=True, vmem_limit_bytes=24 << 20
        ),
        name="up_and_exchange",
    )(strengths, counts, smap, mg)


def take_lanes(x, index):
    dims = lax.GatherDimensionNumbers(
        offset_dims=(),
        collapsed_slice_dims=(1,),
        start_index_map=(1,),
        operand_batching_dims=(0,),
        start_indices_batching_dims=(0,),
    )
    return lax.gather(
        x, index[..., None], dims, slice_sizes=(1, 1), mode=lax.GatherScatterMode.PROMISE_IN_BOUNDS
    )


def far_kernel(
    leaf_w, mid_w, tops, leaf_lists, par_l, gra_l, top_l, tr, sp, out,
    w4, pwin, gwin, twin, g_ref, a_ref, s_ref, ml_ref, mt_ref, acc_ref,
):
    nclass = leaf_lists.shape[0]
    w4[...] = jnp.concatenate([leaf_w[h].astype(F32)[0:ROWS] for h in range(4)], axis=0).astype(BF)
    at = lax.broadcasted_iota(jnp.int16, (16, 128), 1)
    for v in range(7):
        rows = slice(16 * v, 16 * v + 16)
        low, own, high = mid_w[0, rows, :], mid_w[1, rows, :], mid_w[2, rows, :]
        pwin[rows, :] = jnp.where(
            at < 32,
            take_lanes(low, (at + jnp.int16(32)) & jnp.int16(127)),
            jnp.where(
                at < 96,
                take_lanes(own, (at - jnp.int16(32)) & jnp.int16(127)),
                take_lanes(high, (at - jnp.int16(96)) & jnp.int16(127)),
            ),
        )
        gwin[rows, :] = jnp.where(
            at < 4,
            take_lanes(low, (at + jnp.int16(68)) & jnp.int16(127)),
            jnp.where(
                at < 12,
                take_lanes(own, (at + jnp.int16(60)) & jnp.int16(127)),
                take_lanes(high, (at + jnp.int16(52)) & jnp.int16(127)),
            ),
        )
    for i in range(2):
        twin[:, 128 * i : 128 * i + 128] = tops[128 * i : 128 * i + 128, :].T[0:112].astype(BF)
    g_ref[...] = jnp.zeros_like(g_ref)
    a_ref[...] = jnp.zeros_like(a_ref)
    s_ref[...] = jnp.zeros_like(s_ref)
    acc_ref[...] = jnp.zeros_like(acc_ref)
    ml_ref[...] = jnp.full_like(ml_ref, -1)
    ml_ref[0:64, 0:nclass] = par_l[...]
    ml_ref[64:72, 0:nclass] = gra_l[...]
    t = top_l[...]
    ml_ref[72:73, 0:nclass] = jnp.where(t >= 0, (t & 31) * 8 + (t >> 5), -1)
    mt_ref[0:128, :] = ml_ref[:, 0:128].T
    mt_ref[128:256, :] = ml_ref[:, 128:256].T
    for q in range(98):
        s_ref[pl.ds(q, 8, stride=ROWS), 0:98] = sp[q].astype(F32)

    sub = lax.broadcasted_iota(jnp.int16, (16, 512), 0)
    lane = lax.broadcasted_iota(jnp.int32, (16, 128), 1)

    def leaf_class(row, base):
        lo = jnp.broadcast_to(row & 255, (16, 512)).astype(jnp.int16)
        hi = row >> 8
        onehot = jnp.concatenate(
            [
                jnp.where(lo - jnp.int16(16 * g) == sub, BF(1), BF(0))
                for g in range(16)
            ],
            axis=0,
        )
        r = jnp.dot(w4[...], onehot, preferred_element_type=F32)
        picked = jnp.zeros((ROWS, 512), F32)
        for h in range(4):
            hit = jnp.broadcast_to(hi == h, (ROWS, 512))
            picked = jnp.where(hit, r[h * ROWS : (h + 1) * ROWS], picked)
        g_ref[base : base + ROWS, 0:512] = picked.astype(BF)

    def mid_class(row, base):
        e = jnp.broadcast_to(row, (16, 128))
        lo = (e & 127).astype(jnp.int16)
        is_p = ((lane < 64) & (e >= 0)).astype(jnp.int16) > 0
        is_g = ((lane >= 64) & (lane < 72) & (e >= 0)).astype(jnp.int16) > 0
        is_t0 = ((lane == 72) & (e >= 0) & (e < 128)).astype(jnp.int16) > 0
        is_t1 = ((lane == 72) & (e >= 128)).astype(jnp.int16) > 0
        for v in range(7):
            rows = slice(16 * v, 16 * v + 16)
            x = jnp.zeros((16, 128), BF)
            x = jnp.where(is_p, take_lanes(pwin[rows, :], lo), x)
            x = jnp.where(is_g, take_lanes(gwin[rows, :], lo), x)
            x = jnp.where(is_t0, take_lanes(twin[rows, 0:128], lo), x)
            x = jnp.where(is_t1, take_lanes(twin[rows, 128:256], lo), x)
            g_ref[base + 16 * v : base + 16 * v + 16, 512:640] = x

    def group(k0, n):
        for q in range(98):
            a_ref[pl.ds(q, n, stride=ROWS), 0:98] = tr[q, pl.ds(k0, n), :].astype(F32)
        lists = [leaf_lists[pl.ds(k0 + s, min(8, n - s)), :] for s in range(0, n, 8)]
        mids = [mt_ref[pl.ds(k0 + s, min(8, n - s)), :] for s in range(0, n, 8)]
        for c in range(n):
            leaf_class(lists[c // 8][c % 8 : c % 8 + 1], c * 128)
            mid_class(mids[c // 8][c % 8 : c % 8 + 1], c * 128)
        for s in range(0, n, 8):
            m = min(8, n - s)
            ops = jnp.concatenate(
                [a_ref[(s + c) * ROWS : (s + c + 1) * ROWS, :].astype(BF) for c in range(m)], axis=1
            )
            acc_ref[...] += jnp.dot(
                ops, g_ref[s * 128 : (s + m) * 128, :], preferred_element_type=F32
            )

    full = nclass // 16

    def step(j, carry):
        group(pl.multiple_of(j * 16, 16), 16)
        return carry

    lax.fori_loop(0, full, step, 0)
    group(full * 16, nclass - full * 16)

    spread = s_ref[...].astype(BF)
    lane = lax.broadcasted_iota(jnp.int32, (ROWS, 128), 1)

    def spread_from(x, index):
        picked = take_lanes(x, index).astype(BF)
        z = jnp.dot(
            spread,
            jnp.concatenate([picked, jnp.zeros((128 - ROWS, 128), BF)], axis=0),
            preferred_element_type=F32,
        )
        r = z[0:ROWS]
        for c in range(1, 8):
            r = jnp.where((lane & 7) == c, z[c * ROWS : (c + 1) * ROWS], r)
        return r

    mid = acc_ref[:, 512:640]
    grand = 0.25 * mid + spread_from(0.125 * mid, jnp.full((ROWS, 128), 72, jnp.int32))
    parent = 0.5 * mid + spread_from(grand, 64 + ((lane >> 3) & 7))
    for g in range(4):
        cols = slice(128 * g, 128 * g + 128)
        out[:, cols] = (acc_ref[:, cols] + spread_from(parent, 16 * g + (lane >> 3)))[0:98]


def far_all(leaf_w, mid_w, tops, leaf_lists, par_l, gra_l, top_l, tr, sp):
    p, nclass, leaves = tr.shape[0], tr.shape[1], leaf_lists.shape[1]
    vmem = pl.BlockSpec(memory_space=pltpu.VMEM)
    return pl.pallas_call(
        far_kernel,
        out_shape=jax.ShapeDtypeStruct((p, leaves), F32),
        in_specs=[vmem] * 9,
        out_specs=vmem,
        scratch_shapes=[
            pltpu.VMEM((4 * ROWS, 256), BF),
            pltpu.VMEM((112, 128), BF),
            pltpu.VMEM((112, 128), BF),
            pltpu.VMEM((112, 256), BF),
            pltpu.VMEM((16 * 128, 640), BF),
            pltpu.VMEM((16 * ROWS, 128), F32),
            pltpu.VMEM((8 * ROWS, 128), F32),
            pltpu.VMEM((128, 256), jnp.int32),
            pltpu.VMEM((256, 128), jnp.int32),
            pltpu.VMEM((ROWS, 640), F32),
        ],
        compiler_params=pltpu.CompilerParams(vmem_limit_bytes=40 << 20),
        name="far_field",
    )(leaf_w, mid_w, tops, leaf_lists, par_l, gra_l, top_l, tr, sp)


def solution(mesh):
    def per_device(
        strengths, source_counts, source_map, merge_ops, translate_ops, spread_ops,
        leaf_lists, parent_lists, grand_lists, top_lists,
    ):
        leaf_w, mid_w, tops = go_up(
            mesh, strengths, source_counts.reshape(1, -1), source_map.T, merge_ops.transpose(1, 0, 2)
        )
        return far_all(
            leaf_w, mid_w, tops.reshape(-1, 128), leaf_lists, parent_lists.T, grand_lists.T, top_lists.T,
            translate_ops.transpose(1, 0, 2), spread_ops.transpose(1, 0, 2),
        )

    spread_out = P(("grp", "dev"))
    cols = P(None, ("grp", "dev"))
    return jax.shard_map(
        per_device,
        mesh=mesh,
        in_specs=(P(("grp", "dev"), None), spread_out, P(), P(), P(), P(), cols, cols, cols, cols),
        out_specs=cols,
        check_vma=False,
    )
```

time: 524 us -> 65.1 us (0.12)
  local copies, waits for them, and re-layouts: 400 us -> 9.86 us
  Pallas kernels: 0 us -> 54.8 us
  blocking collectives: 54 us -> 0 us
  starting transfers between devices: 29.9 us -> 0 us
  matrix products: 22.8 us -> 0 us
  other arithmetic: 15.2 us -> 0 us
    gather x17 -> x0, local copies, waits for them, and re-layouts: 378 us -> none  [the longest x16 377 us: translate_window(): picked = jnp.take(padded, offset, axis=1)]
    pallas_call x0 -> x2, Pallas kernels: none -> 54.8 us  [the longest x1 32.3 us: far_all(): pl.pallas_call(far_kernel, out_shape=jax.ShapeDtypeStruct((p, leaves), F3...]
    all_gather x1 -> x0, blocking collectives: 54 us -> none  [per_device(): piece_rows = lax.all_gather(top_m, ('grp', 'dev'), axis=1, tiled=True)]
    ppermute x6 -> x0, starting transfers between devices: 29.9 us -> none  [from_behind(): return lax.ppermute(block, axis, route)]
    dot_general x17 -> x0, matrix products: 22.8 us -> none  [the longest x10 13.5 us: translate_window(): jnp.einsum('kqp,pkn->qn', operators[first_class:first_class + block_size]...]
    slice x5 -> x0, local copies, waits for them, and re-layouts: 8.85 us -> none  [the longest x2 7 us: translate_window(): operators[first_class:first_class + block_size]]
    gather x13 -> x0, other arithmetic: 6.84 us -> none
  transfers between devices with their start and end apart: 6 -> 0, of which waited for: 0 -> 0; matrix products, arithmetic and copies ran while one was open for 16% -> 0% of each run, Pallas kernels for 0% -> 0%
where the time goes in v1:
time: 65.1 us; the launch traced here: 64.7 us
  Pallas kernels  54.8 us (84%)
  local copies, waits for them, and re-layouts  9.86 us (15%)
    pallas_call x1, Pallas kernels, far_all(): pl.pallas_call(far_kernel, out_shape=jax.ShapeDtypeStruct((p, leaves), F3...  32.3 us
    pallas_call x1, Pallas kernels, go_up(): pl.pallas_call(lambda *refs: up_kernel(grps, devs, *refs), out_shape=(jax...  22.5 us
    unnamed x20, local copies, waits for them, and re-layouts  9.86 us

profile of v1, /device:TPU:1, one launch (start us, length us, event | category | flops | bytes accessed | tf_op | source)
XLA Modules:
  0.0 64.7 jit_solution(11765025190441349268)
XLA Ops:
  0.0 0.0 copy-start.2
  0.0 0.9 %copy-done.2 = bf16[512,256]{1,0:T(8,128)(2,1)S(1)} copy-done((bf16[512,256]{1,0:T(8,128)(2,1)S(1)}, bf16[512,256]{1,0:T(8,128)(2,1)}, u32[]{:S(2)}) %copy-start.2) | copy-done | bytes 262168
  1.0 0.0 copy-start.4
  1.0 0.9 %copy-done.4 = bf16[8,98,98]{2,0,1:T(8,128)(2,1)S(1)} copy-done((bf16[8,98,98]{2,0,1:T(8,128)(2,1)S(1)}, bf16[8,98,98]{2,0,1:T(8,128)(2,1)}, u32[]{:S(2)}) %copy-start.4) | copy-done | bytes 153688
  1.9 0.0 copy-start.6
  1.9 0.8 %copy-done.6 = bf16[256,98]{0,1:T(8,128)(2,1)S(1)} copy-done((bf16[256,98]{0,1:T(8,128)(2,1)S(1)}, bf16[256,98]{0,1:T(8,128)(2,1)}, u32[]{:S(2)}) %copy-start.6) | copy-done | bytes 50200
  2.7 0.0 copy-start.8
  2.7 0.7 %copy-done.8 = s32[512]{0:T(512)S(1)} copy-done((s32[512]{0:T(512)S(1)}, s32[512]{0:T(512)}, u32[]{:S(2)}) %copy-start.8) | copy-done | bytes 2072
  3.4 22.5 %up_and_exchange.1 = (bf16[4,112,256]{2,1,0:T(8,128)(2,1)S(1)}, bf16[3,112,128]{2,1,0:T(8,128)(2,1)S(1)}, f32[32,8,128]{2,1,0:T(8,128)S(1)}) custom-call(bf16[512,256]{1,0:T(8,128)(2,1)S(1)} %copy-done.2, s32[1,512]{1,0:T(1,128)S(1)} %bitcast.16, bf16[98,256]{1,0:T(8,128)(2,1)S(1)} %bitcast.14, bf16[98,8,98]{2,1,0:T(8,128)(2,1)S(1)} %bitcast.11), custom_call_target="tpu_custom_call" | custom-call | tf_op jit(solution)/shard_map/up_and_exchange/pallas_call | solution.py:147
  25.9 0.0 copy-start
  25.9 2.4 %copy-done = bf16[189,98,98]{2,0,1:T(8,128)(2,1)S(1)} copy-done((bf16[189,98,98]{2,0,1:T(8,128)(2,1)S(1)}, bf16[189,98,98]{2,0,1:T(8,128)(2,1)}, u32[]{:S(2)}) %copy-start) | copy-done | bytes 3630336
  28.2 0.0 copy-start.1
  28.2 1.0 %copy-done.1 = s32[189,512]{1,0:T(8,128)S(1)} copy-done((s32[189,512]{1,0:T(8,128)S(1)}, s32[189,512]{1,0:T(8,128)}, u32[]{:S(2)}) %copy-start.1) | copy-done | bytes 387096
  29.2 0.0 copy-start.3
  29.2 0.9 %copy-done.3 = bf16[8,98,98]{2,0,1:T(8,128)(2,1)S(1)} copy-done((bf16[8,98,98]{2,0,1:T(8,128)(2,1)S(1)}, bf16[8,98,98]{2,0,1:T(8,128)(2,1)}, u32[]{:S(2)}) %copy-start.3) | copy-done | bytes 153688
  30.2 0.0 copy-start.5
  30.2 0.8 %copy-done.5 = s32[189,64]{0,1:T(8,128)S(1)} copy-done((s32[189,64]{0,1:T(8,128)S(1)}, s32[189,64]{0,1:T(8,128)}, u32[]{:S(2)}) %copy-start.5) | copy-done | bytes 48408
  31.0 0.0 copy-start.7
  31.0 0.7 %copy-done.7 = s32[189,8]{0,1:T(8,128)S(1)} copy-done((s32[189,8]{0,1:T(8,128)S(1)}, s32[189,8]{0,1:T(8,128)}, u32[]{:S(2)}) %copy-start.7) | copy-done | bytes 6072
  31.7 0.0 copy-start.9
  31.7 0.7 %copy-done.9 = s32[189,1]{0,1:T(1,128)S(1)} copy-done((s32[189,1]{0,1:T(1,128)S(1)}, s32[189,1]{0,1:T(1,128)}, u32[]{:S(2)}) %copy-start.9) | copy-done | bytes 780
  32.4 32.3 %far_field.1 = f32[98,512]{1,0:T(8,128)} custom-call(bf16[4,112,256]{2,1,0:T(8,128)(2,1)S(1)} %get-tuple-element.8.leaf_w, bf16[3,112,128]{2,1,0:T(8,128)(2,1)S(1)} %get-tuple-element.9.mid_w, f32[256,128]{1,0:T(8,128)S(1)} %bitcast.12, s32[189,512]{1,0:T(8,128)S(1)} %copy-done.1, s32[64,189]{1,0:T(8,128)S(1)} %bitcast.13, s32[8,189]{1,0:T(8,128)S(1)} %bitcast.15, ...), custom_call_target="tpu_custom_call" | custom-call | tf_op jit(solution)/shard_map/far_field/pallas_call | solution.py:324
Async XLA Ops:
  0.0 0.9 %copy-start.2 = (bf16[512,256]{1,0:T(8,128)(2,1)S(1)}, bf16[512,256]{1,0:T(8,128)(2,1)}, u32[]{:S(2)}) copy-start(bf16[512,256]{1,0:T(8,128)(2,1)} %refs_0_.1) | copy-start | bytes 786436
  1.0 0.9 %copy-start.4 = (bf16[8,98,98]{2,0,1:T(8,128)(2,1)S(1)}, bf16[8,98,98]{2,0,1:T(8,128)(2,1)}, u32[]{:S(2)}) copy-start(bf16[8,98,98]{2,0,1:T(8,128)(2,1)} %param.13) | copy-start | bytes 460996
  1.9 0.8 %copy-start.6 = (bf16[256,98]{0,1:T(8,128)(2,1)S(1)}, bf16[256,98]{0,1:T(8,128)(2,1)}, u32[]{:S(2)}) copy-start(bf16[256,98]{0,1:T(8,128)(2,1)} %param.12) | copy-start | bytes 150532
  2.7 0.7 %copy-start.8 = (s32[512]{0:T(512)S(1)}, s32[512]{0:T(512)}, u32[]{:S(2)}) copy-start(s32[512]{0:T(512)} %param.11) | copy-start | bytes 6148
  25.9 2.4 %copy-start = (bf16[189,98,98]{2,0,1:T(8,128)(2,1)S(1)}, bf16[189,98,98]{2,0,1:T(8,128)(2,1)}, u32[]{:S(2)}) copy-start(bf16[189,98,98]{2,0,1:T(8,128)(2,1)} %param.14) | copy-start | bytes 10890940
  28.2 1.0 %copy-start.1 = (s32[189,512]{1,0:T(8,128)S(1)}, s32[189,512]{1,0:T(8,128)}, u32[]{:S(2)}) copy-start(s32[189,512]{1,0:T(8,128)} %leaf_lists.1) | copy-start | bytes 1161220
  29.2 0.9 %copy-start.3 = (bf16[8,98,98]{2,0,1:T(8,128)(2,1)S(1)}, bf16[8,98,98]{2,0,1:T(8,128)(2,1)}, u32[]{:S(2)}) copy-start(bf16[8,98,98]{2,0,1:T(8,128)(2,1)} %param.15) | copy-start | bytes 460996
  30.2 0.8 %copy-start.5 = (s32[189,64]{0,1:T(8,128)S(1)}, s32[189,64]{0,1:T(8,128)}, u32[]{:S(2)}) copy-start(s32[189,64]{0,1:T(8,128)} %param.17) | copy-start | bytes 145156
  31.0 0.7 %copy-start.7 = (s32[189,8]{0,1:T(8,128)S(1)}, s32[189,8]{0,1:T(8,128)}, u32[]{:S(2)}) copy-start(s32[189,8]{0,1:T(8,128)} %param.18) | copy-start | bytes 18148
  31.7 0.7 %copy-start.9 = (s32[189,1]{0,1:T(1,128)S(1)}, s32[189,1]{0,1:T(1,128)}, u32[]{:S(2)}) copy-start(s32[189,1]{0,1:T(1,128)} %param.19) | copy-start | bytes 2272

commit v2 on v1

v2 whole, which is shorter than its diff:
```python
import jax
import jax.numpy as jnp
from jax import lax
from jax.experimental import pallas as pl
from jax.experimental.pallas import tpu as pltpu
from jax.sharding import PartitionSpec as P

BF = jnp.bfloat16
F32 = jnp.float32
ROWS = 104
MESH = pl.DeviceIdType.MESH
NT = (((1,), (1,)), ((), ()))


def take_lanes(x, index):
    dims = lax.GatherDimensionNumbers(
        offset_dims=(),
        collapsed_slice_dims=(1,),
        start_index_map=(1,),
        operand_batching_dims=(0,),
        start_indices_batching_dims=(0,),
    )
    return lax.gather(
        x, index[..., None], dims, slice_sizes=(1, 1), mode=lax.GatherScatterMode.PROMISE_IN_BOUNDS
    )


def kernel(
    grps, devs,
    strengths_h, counts_h, smap_h, mg_h, leaf_lists_h, par_h, gra_h, top_h, tr_h, sp_h, out,
    strengths, counts, smap, mg, leaf_lists, par_l, gra_l, top_l, tr, sp,
    m_ref, leaf_t, par_t, gra_t, mine, got, midm, midg, msg, buf_a, msg_b, buf_b, tops,
    w4, pwin, gwin, g_ref, a_ref, s_ref, ml_ref, mt_ref, acc_ref, tsum_ref,
    load_sem, send_l, recv_l, send_m, recv_m, send_a, recv_a, send_b, recv_b,
):
    g = lax.axis_index("grp")
    d = lax.axis_index("dev")
    total = grps * devs
    me = g * devs + d
    above = lax.rem(me + 1, total)
    below = lax.rem(me + total - 1, total)

    def at(pos):
        return (pos // devs, lax.rem(pos, devs))

    def load(src, dst, k):
        c = pltpu.make_async_copy(src, dst, load_sem.at[k])
        c.start()
        return c

    strengths_in = load(strengths_h, strengths, 0)
    counts_in = load(counts_h, counts, 1)
    smap_in = load(smap_h, smap, 2)
    mg_in = load(mg_h, mg, 3)
    lists_in = [
        load(h, v, 4 + i)
        for i, (h, v) in enumerate(
            ((leaf_lists_h, leaf_lists), (par_h, par_l), (gra_h, gra_l), (top_h, top_l), (sp_h, sp))
        )
    ]
    tr_in = load(tr_h, tr, 9)
    barrier = pltpu.get_barrier_semaphore()

    def greet(pos):
        pl.semaphore_signal(barrier, inc=1, device_id=pos, device_id_type=MESH)

    greet(at(above))
    greet(at(below))
    lax.fori_loop(1, grps, lambda i, c: (greet((lax.rem(g + i, grps), d)), c)[1], 0)
    lax.fori_loop(1, devs, lambda i, c: (greet((g, lax.rem(d + i, devs))), c)[1], 0)

    for r in (leaf_t, par_t, gra_t, m_ref, a_ref, s_ref, acc_ref, tsum_ref):
        r[...] = jnp.zeros_like(r)
    g_ref[...] = jnp.zeros_like(g_ref)
    ml_ref[...] = jnp.full_like(ml_ref, -1)
    for r in (strengths_in, counts_in, smap_in):
        r.wait()
    cnt = jnp.concatenate(
        [jnp.broadcast_to(counts[:, 128 * i : 128 * i + 128], (128, 128)).T for i in range(4)], axis=0
    ).astype(jnp.int16)
    slot = lax.broadcasted_iota(jnp.int16, (512, 128), 1)
    zero = jnp.zeros((512, 128), BF)
    live = jnp.concatenate(
        [
            jnp.where(slot < cnt, strengths[:, 0:128], zero),
            jnp.where(slot + jnp.int16(128) < cnt, strengths[:, 128:256], zero),
        ],
        axis=1,
    )
    lt = lax.dot_general(live, smap[...], NT, preferred_element_type=F32)
    leaf_t[:, 0:98] = lt.astype(BF).astype(F32)
    for half in range(2):
        mine[half] = jnp.concatenate(
            [leaf_t[256 * half + 128 * i : 256 * half + 128 * i + 128, :].T[0:112] for i in range(2)], axis=1
        ).astype(BF)

    def copy(src, dst, ss, rs, pos):
        return pltpu.make_async_remote_copy(
            src_ref=src, dst_ref=dst, send_sem=ss, recv_sem=rs, device_id=pos, device_id_type=MESH
        )

    pl.semaphore_wait(barrier, 2 + grps - 1 + devs - 1)
    leaf_up = copy(mine.at[1], got.at[0], send_l.at[0], recv_l.at[0], at(above))
    leaf_dn = copy(mine.at[0], got.at[1], send_l.at[1], recv_l.at[1], at(below))
    leaf_up.start()
    leaf_dn.start()

    mg_in.wait()
    for q in range(98):
        m_ref[pl.ds(q, 8, stride=ROWS), 0:98] = mg[q].astype(F32)
    merge = jnp.concatenate([m_ref[ROWS * c : ROWS * c + ROWS, :].astype(BF) for c in range(8)], axis=1)

    def merged(kids):
        x = jnp.concatenate([k.astype(BF) for k in kids], axis=1)
        y = lax.dot_general(x, merge, NT, preferred_element_type=F32)
        return y.astype(BF).astype(F32)

    par_t[:, 0:ROWS] = merged([leaf_t[pl.ds(c, 64, stride=8), :] for c in range(8)])
    gra_t[:, 0:ROWS] = merged([par_t[pl.ds(c, 8, stride=8), :] for c in range(8)])
    msg[...] = jnp.zeros_like(msg)
    msg[:, 0:ROWS] = merged([jnp.broadcast_to(gra_t[c : c + 1, :], (8, 128)) for c in range(8)])

    def send_top(i, c):
        to = lax.rem(g + i, grps)
        copy(msg, buf_a.at[g], send_a.at[i], recv_a.at[g], (to, d)).start()
        return c

    lax.fori_loop(1, grps, send_top, 0)

    both = jnp.concatenate([par_t[...], gra_t[...], jnp.zeros((56, 128), F32)], axis=0)
    midm[...] = both.T[0:112].astype(BF)
    mid_up = copy(midm, midg.at[0], send_m.at[0], recv_m.at[0], at(above))
    mid_dn = copy(midm, midg.at[1], send_m.at[1], recv_m.at[1], at(below))
    mid_up.start()
    mid_dn.start()

    nclass = leaf_lists.shape[0]
    leaf_up.wait()
    leaf_dn.wait()
    w4[...] = jnp.concatenate(
        [b.astype(F32)[0:ROWS] for b in (got[0], mine[0], mine[1], got[1])], axis=0
    ).astype(BF)
    mid_up.wait()
    mid_dn.wait()
    at = lax.broadcasted_iota(jnp.int16, (16, 128), 1)
    for v in range(7):
        rows = slice(16 * v, 16 * v + 16)
        low, own, high = midg[0, rows, :], midm[rows, :], midg[1, rows, :]
        pwin[rows, :] = jnp.where(
            at < 32,
            take_lanes(low, (at + jnp.int16(32)) & jnp.int16(127)),
            jnp.where(
                at < 96,
                take_lanes(own, (at - jnp.int16(32)) & jnp.int16(127)),
                take_lanes(high, (at - jnp.int16(96)) & jnp.int16(127)),
            ),
        )
        gwin[rows, :] = jnp.where(
            at < 4,
            take_lanes(low, (at + jnp.int16(68)) & jnp.int16(127)),
            jnp.where(
                at < 12,
                take_lanes(own, (at + jnp.int16(60)) & jnp.int16(127)),
                take_lanes(high, (at + jnp.int16(52)) & jnp.int16(127)),
            ),
        )
    for r in lists_in:
        r.wait()
    ml_ref[0:64, 0:nclass] = par_l[...]
    ml_ref[64:72, 0:nclass] = gra_l[...]
    mt_ref[0:128, :] = ml_ref[:, 0:128].T
    mt_ref[128:256, :] = ml_ref[:, 128:256].T
    for q in range(98):
        s_ref[pl.ds(q, 8, stride=ROWS), 0:98] = sp[q].astype(F32)

    tr_in.wait()
    sub = lax.broadcasted_iota(jnp.int32, (8, 128), 0)

    def wait_top(i, c):
        frm = lax.rem(g + i, grps)
        w = copy(msg, buf_a.at[frm], send_a.at[i], recv_a.at[frm], (frm, d))
        w.wait_send()
        w.wait_recv()
        return jnp.where(sub == frm, buf_a[frm], c)

    msg_b[...] = lax.fori_loop(1, grps, wait_top, msg[...])

    def send_block(i, c):
        to = lax.rem(d + i, devs)
        copy(msg_b, buf_b.at[d], send_b.at[i], recv_b.at[d], (g, to)).start()
        return c

    lax.fori_loop(1, devs, send_block, 0)
    sub = lax.broadcasted_iota(jnp.int16, (16, 512), 0)
    lane = lax.broadcasted_iota(jnp.int32, (16, 128), 1)

    def leaf_class(row, base):
        lo = jnp.broadcast_to(row & 255, (16, 512)).astype(jnp.int16)
        hi = row >> 8
        onehot = jnp.concatenate(
            [
                jnp.where(lo - jnp.int16(16 * g) == sub, BF(1), BF(0))
                for g in range(16)
            ],
            axis=0,
        )
        r = jnp.dot(w4[...], onehot, preferred_element_type=F32)
        picked = jnp.zeros((ROWS, 512), F32)
        for h in range(4):
            hit = jnp.broadcast_to(hi == h, (ROWS, 512))
            picked = jnp.where(hit, r[h * ROWS : (h + 1) * ROWS], picked)
        g_ref[base : base + ROWS, 0:512] = picked.astype(BF)

    def mid_class(row, base):
        e = jnp.broadcast_to(row, (16, 128))
        lo = (e & 127).astype(jnp.int16)
        is_p = ((lane < 64) & (e >= 0)).astype(jnp.int16) > 0
        is_g = ((lane >= 64) & (lane < 72) & (e >= 0)).astype(jnp.int16) > 0
        for v in range(7):
            rows = slice(16 * v, 16 * v + 16)
            x = jnp.zeros((16, 128), BF)
            x = jnp.where(is_p, take_lanes(pwin[rows, :], lo), x)
            x = jnp.where(is_g, take_lanes(gwin[rows, :], lo), x)
            g_ref[base + 16 * v : base + 16 * v + 16, 512:640] = x

    def group(k0, n):
        for q in range(98):
            a_ref[pl.ds(q, n, stride=ROWS), 0:98] = tr[q, pl.ds(k0, n), :].astype(F32)
        lists = [leaf_lists[pl.ds(k0 + s, min(8, n - s)), :] for s in range(0, n, 8)]
        mids = [mt_ref[pl.ds(k0 + s, min(8, n - s)), :] for s in range(0, n, 8)]
        for c in range(n):
            leaf_class(lists[c // 8][c % 8 : c % 8 + 1], c * 128)
            mid_class(mids[c // 8][c % 8 : c % 8 + 1], c * 128)
        for s in range(0, n, 8):
            m = min(8, n - s)
            ops = jnp.concatenate(
                [a_ref[(s + c) * ROWS : (s + c + 1) * ROWS, :].astype(BF) for c in range(m)], axis=1
            )
            acc_ref[...] += jnp.dot(
                ops, g_ref[s * 128 : (s + m) * 128, :], preferred_element_type=F32
            )

    full = nclass // 16

    def step(j, carry):
        group(pl.multiple_of(j * 16, 16), 16)
        return carry

    lax.fori_loop(0, full, step, 0)
    group(full * 16, nclass - full * 16)

    def wait_block(i, c):
        frm = lax.rem(d + i, devs)
        w = copy(msg_b, buf_b.at[frm], send_b.at[i], recv_b.at[frm], (g, frm))
        w.wait_send()
        w.wait_recv()
        tops[frm] = buf_b[frm]
        return c

    tops[d] = msg_b[...]
    lax.fori_loop(1, devs, wait_block, 0)
    t = top_l[...]
    t = jnp.broadcast_to(jnp.where(t >= 0, (t & 31) * 8 + (t >> 5), -1), (256, nclass))
    hits = jnp.where(lax.broadcasted_iota(jnp.int32, (256, nclass), 0) == t, 1.0, 0.0).astype(BF)
    table = tops[...].reshape(256, 128).astype(BF)
    named = lax.dot_general(hits, table, (((0,), (0,)), ((), ())), preferred_element_type=F32)[:, 0:98]
    for q in range(98):
        tsum_ref[q : q + 1, 0:98] = jnp.sum(tr[q].astype(F32) * named, axis=0, keepdims=True)
    top = jnp.broadcast_to(0.125 * jnp.sum(tsum_ref[...], axis=1, keepdims=True), (ROWS, 128))

    spread = s_ref[...].astype(BF)
    lane = lax.broadcasted_iota(jnp.int32, (ROWS, 128), 1)

    def spread_from(x, index):
        picked = (x if index is None else take_lanes(x, index)).astype(BF)
        z = jnp.dot(
            spread,
            jnp.concatenate([picked, jnp.zeros((128 - ROWS, 128), BF)], axis=0),
            preferred_element_type=F32,
        )
        r = z[0:ROWS]
        for c in range(1, 8):
            r = jnp.where((lane & 7) == c, z[c * ROWS : (c + 1) * ROWS], r)
        return r

    mid = acc_ref[:, 512:640]
    grand = 0.25 * mid + spread_from(top, None)
    parent = 0.5 * mid + spread_from(grand, 64 + ((lane >> 3) & 7))
    for g in range(4):
        cols = slice(128 * g, 128 * g + 128)
        out[:, cols] = (acc_ref[:, cols] + spread_from(parent, 16 * g + (lane >> 3)))[0:98]


def solution(mesh):
    grps, devs = mesh.shape["grp"], mesh.shape["dev"]

    def per_device(
        strengths, source_counts, source_map, merge_ops, translate_ops, spread_ops,
        leaf_lists, parent_lists, grand_lists, top_lists,
    ):
        args = (
            strengths, source_counts.reshape(1, -1), source_map.T, merge_ops.transpose(1, 0, 2),
            leaf_lists, parent_lists.T, grand_lists.T, top_lists.T,
            translate_ops.transpose(1, 0, 2), spread_ops.transpose(1, 0, 2),
        )
        dma = pltpu.SemaphoreType.DMA
        vm = pltpu.VMEM
        return pl.pallas_call(
            lambda *refs: kernel(grps, devs, *refs),
            out_shape=jax.ShapeDtypeStruct((98, leaf_lists.shape[1]), F32),
            in_specs=[pl.BlockSpec(memory_space=pl.ANY)] * len(args),
            out_specs=pl.BlockSpec(memory_space=pltpu.VMEM),
            scratch_shapes=[vm(a.shape, a.dtype) for a in args]
            + [
                vm((8 * ROWS, 128), F32),
                vm((512, 128), F32),
                vm((64, 128), F32),
                vm((8, 128), F32),
                vm((2, 112, 256), BF),
                vm((2, 112, 256), BF),
                vm((112, 128), BF),
                vm((2, 112, 128), BF),
                vm((8, 128), F32),
                vm((grps, 8, 128), F32),
                vm((8, 128), F32),
                vm((devs, 8, 128), F32),
                vm((devs, 8, 128), F32),
                vm((4 * ROWS, 256), BF),
                vm((112, 128), BF),
                vm((112, 128), BF),
                vm((16 * 128, 640), BF),
                vm((16 * ROWS, 128), F32),
                vm((8 * ROWS, 128), F32),
                vm((128, 256), jnp.int32),
                vm((256, 128), jnp.int32),
                vm((ROWS, 640), F32),
                vm((ROWS, 128), F32),
                dma((10,)),
                dma((2,)), dma((2,)), dma((2,)), dma((2,)),
                dma((grps,)), dma((grps,)), dma((devs,)), dma((devs,)),
            ],
            compiler_params=pltpu.CompilerParams(
                collective_id=0, has_side_effects=True, vmem_limit_bytes=48 << 20
            ),
            name="fmm",
        )(*args)

    rows = P(("grp", "dev"))
    cols = P(None, ("grp", "dev"))
    return jax.shard_map(
        per_device,
        mesh=mesh,
        in_specs=(P(("grp", "dev"), None), rows, P(), P(), P(), P(), cols, cols, cols, cols),
        out_specs=cols,
        check_vma=False,
    )
```

time: 65.1 us -> 63 us (0.968)
  Pallas kernels: 54.8 us -> 52 us
  local copies, waits for them, and re-layouts: 9.86 us -> 10.6 us
    pallas_call x2 -> x1, Pallas kernels: 54.8 us -> 52 us  [per_device(): pl.pallas_call(lambda *refs: kernel(grps, devs, *refs), out_shape=jax.Sha...]
    unnamed x20 -> x21, local copies, waits for them, and re-layouts: 9.86 us -> 10.6 us
where the time goes in v2:
time: 63 us; the launch traced here: 62.6 us
  Pallas kernels  52 us (83%)
  local copies, waits for them, and re-layouts  10.6 us (17%)
    pallas_call x1, Pallas kernels, per_device(): pl.pallas_call(lambda *refs: kernel(grps, devs, *refs), out_shape=jax.Sha...  52 us
    unnamed x21, local copies, waits for them, and re-layouts  10.6 us

profile of v2, /device:TPU:1, one launch (start us, length us, event | category | flops | bytes accessed | tf_op | source)
XLA Modules:
  0.0 62.6 jit_solution(6218891119174715427)
XLA Ops:
  0.0 0.0 copy-start
  0.0 2.4 %copy-done = bf16[189,98,98]{2,0,1:T(8,128)(2,1)S(1)} copy-done((bf16[189,98,98]{2,0,1:T(8,128)(2,1)S(1)}, bf16[189,98,98]{2,0,1:T(8,128)(2,1)}, u32[]{:S(2)}) %copy-start) | copy-done | bytes 3630336
  2.4 0.0 copy-start.1
  2.4 1.0 %copy-done.1 = s32[189,512]{1,0:T(8,128)S(1)} copy-done((s32[189,512]{1,0:T(8,128)S(1)}, s32[189,512]{1,0:T(8,128)}, u32[]{:S(2)}) %copy-start.1) | copy-done | bytes 387096
  3.4 0.0 copy-start.2
  3.4 0.9 %copy-done.2 = bf16[512,256]{1,0:T(8,128)(2,1)S(1)} copy-done((bf16[512,256]{1,0:T(8,128)(2,1)S(1)}, bf16[512,256]{1,0:T(8,128)(2,1)}, u32[]{:S(2)}) %copy-start.2) | copy-done | bytes 262168
  4.3 0.0 copy-start.3
  4.3 0.9 %copy-done.3 = bf16[8,98,98]{2,0,1:T(8,128)(2,1)S(1)} copy-done((bf16[8,98,98]{2,0,1:T(8,128)(2,1)S(1)}, bf16[8,98,98]{2,0,1:T(8,128)(2,1)}, u32[]{:S(2)}) %copy-start.3) | copy-done | bytes 153688
  5.2 0.0 copy-start.4
  5.2 0.9 %copy-done.4 = bf16[8,98,98]{2,0,1:T(8,128)(2,1)S(1)} copy-done((bf16[8,98,98]{2,0,1:T(8,128)(2,1)S(1)}, bf16[8,98,98]{2,0,1:T(8,128)(2,1)}, u32[]{:S(2)}) %copy-start.4) | copy-done | bytes 153688
  6.2 0.0 copy-start.5
  6.2 0.8 %copy-done.5 = s32[189,64]{0,1:T(8,128)S(1)} copy-done((s32[189,64]{0,1:T(8,128)S(1)}, s32[189,64]{0,1:T(8,128)}, u32[]{:S(2)}) %copy-start.5) | copy-done | bytes 48408
  7.0 0.0 copy-start.6
  7.0 0.8 %copy-done.6 = bf16[256,98]{0,1:T(8,128)(2,1)S(1)} copy-done((bf16[256,98]{0,1:T(8,128)(2,1)S(1)}, bf16[256,98]{0,1:T(8,128)(2,1)}, u32[]{:S(2)}) %copy-start.6) | copy-done | bytes 50200
  7.8 0.0 copy-start.7
  7.8 0.7 %copy-done.7 = s32[189,8]{0,1:T(8,128)S(1)} copy-done((s32[189,8]{0,1:T(8,128)S(1)}, s32[189,8]{0,1:T(8,128)}, u32[]{:S(2)}) %copy-start.7) | copy-done | bytes 6072
  8.5 0.0 copy-start.8
  8.5 0.7 %copy-done.8 = s32[512]{0:T(512)S(1)} copy-done((s32[512]{0:T(512)S(1)}, s32[512]{0:T(512)}, u32[]{:S(2)}) %copy-start.8) | copy-done | bytes 2072
  9.2 0.0 copy-start.9
  9.2 0.7 %copy-done.9 = s32[189,1]{0,1:T(1,128)S(1)} copy-done((s32[189,1]{0,1:T(1,128)S(1)}, s32[189,1]{0,1:T(1,128)}, u32[]{:S(2)}) %copy-start.9) | copy-done | bytes 780
  9.9 52.0 %fmm.1 = f32[98,512]{1,0:T(8,128)S(1)} custom-call(bf16[512,256]{1,0:T(8,128)(2,1)S(1)} %copy-done.2, s32[1,512]{1,0:T(1,128)S(1)} %bitcast.14, bf16[98,256]{1,0:T(8,128)(2,1)S(1)} %bitcast.12, bf16[98,8,98]{2,1,0:T(8,128)(2,1)S(1)} %bitcast.9, s32[189,512]{1,0:T(8,128)S(1)} %copy-done.1, s32[64,189]{1,0:T(8,128)S(1)} %bitcast.11, s32[8,189]{1,0:T(8,128)S(1)} %bitcast.13, ...), custom_call_target="tpu_custom_call" | custom-call | tf_op jit(solution)/shard_map/fmm/pallas_call | solution.py:308
  61.9 0.7 %copy.12 = f32[98,512]{1,0:T(8,128)} copy(f32[98,512]{1,0:T(8,128)S(1)} %fmm.1) | data formatting | bytes 401408
Async XLA Ops:
  0.0 2.4 %copy-start = (bf16[189,98,98]{2,0,1:T(8,128)(2,1)S(1)}, bf16[189,98,98]{2,0,1:T(8,128)(2,1)}, u32[]{:S(2)}) copy-start(bf16[189,98,98]{2,0,1:T(8,128)(2,1)} %param.14) | copy-start | bytes 10890940
  2.4 1.0 %copy-start.1 = (s32[189,512]{1,0:T(8,128)S(1)}, s32[189,512]{1,0:T(8,128)}, u32[]{:S(2)}) copy-start(s32[189,512]{1,0:T(8,128)} %refs_4_.1) | copy-start | bytes 1161220
  3.4 0.9 %copy-start.2 = (bf16[512,256]{1,0:T(8,128)(2,1)S(1)}, bf16[512,256]{1,0:T(8,128)(2,1)}, u32[]{:S(2)}) copy-start(bf16[512,256]{1,0:T(8,128)(2,1)} %refs_0_.1) | copy-start | bytes 786436
  4.3 0.9 %copy-start.3 = (bf16[8,98,98]{2,0,1:T(8,128)(2,1)S(1)}, bf16[8,98,98]{2,0,1:T(8,128)(2,1)}, u32[]{:S(2)}) copy-start(bf16[8,98,98]{2,0,1:T(8,128)(2,1)} %param.13) | copy-start | bytes 460996
  5.2 0.9 %copy-start.4 = (bf16[8,98,98]{2,0,1:T(8,128)(2,1)S(1)}, bf16[8,98,98]{2,0,1:T(8,128)(2,1)}, u32[]{:S(2)}) copy-start(bf16[8,98,98]{2,0,1:T(8,128)(2,1)} %param.15) | copy-start | bytes 460996
  6.2 0.8 %copy-start.5 = (s32[189,64]{0,1:T(8,128)S(1)}, s32[189,64]{0,1:T(8,128)}, u32[]{:S(2)}) copy-start(s32[189,64]{0,1:T(8,128)} %param.17) | copy-start | bytes 145156
  7.0 0.8 %copy-start.6 = (bf16[256,98]{0,1:T(8,128)(2,1)S(1)}, bf16[256,98]{0,1:T(8,128)(2,1)}, u32[]{:S(2)}) copy-start(bf16[256,98]{0,1:T(8,128)(2,1)} %param.12) | copy-start | bytes 150532
  7.8 0.7 %copy-start.7 = (s32[189,8]{0,1:T(8,128)S(1)}, s32[189,8]{0,1:T(8,128)}, u32[]{:S(2)}) copy-start(s32[189,8]{0,1:T(8,128)} %param.18) | copy-start | bytes 18148
  8.5 0.7 %copy-start.8 = (s32[512]{0:T(512)S(1)}, s32[512]{0:T(512)}, u32[]{:S(2)}) copy-start(s32[512]{0:T(512)} %param.11) | copy-start | bytes 6148
  9.2 0.7 %copy-start.9 = (s32[189,1]{0,1:T(1,128)S(1)}, s32[189,1]{0,1:T(1,128)}, u32[]{:S(2)}) copy-start(s32[189,1]{0,1:T(1,128)} %param.19) | copy-start | bytes 2272

commit v3 on v2

--- a/solution.py
+++ b/solution.py
@@ -9,6 +9,8 @@
 F32 = jnp.float32
 ROWS = 104
 MESH = pl.DeviceIdType.MESH
+ZS = 8
+LANES = (2, 6, 10, 14)
 NT = (((1,), (1,)), ((), ()))
 
 
@@ -29,13 +31,15 @@
     grps, devs,
     strengths_h, counts_h, smap_h, mg_h, leaf_lists_h, par_h, gra_h, top_h, tr_h, sp_h, out,
     strengths, counts, smap, mg, leaf_lists, par_l, gra_l, top_l, tr, sp,
-    m_ref, leaf_t, par_t, gra_t, mine, got, midm, midg, msg, buf_a, msg_b, buf_b, tops,
-    w4, pwin, gwin, g_ref, a_ref, s_ref, ml_ref, mt_ref, acc_ref, tsum_ref,
-    load_sem, send_l, recv_l, send_m, recv_m, send_a, recv_a, send_b, recv_b,
+    m_ref, leaf_t, par_t, gra_t, mine, got, midm, midg, msg, buf_a, msg_b, buf_b, ring, tops,
+    w4, win, pwin, gwin, g_ref, a_ref, s_ref, ml_ref, mt_ref, acc_ref, tsum_ref,
+    load_sem, send_l, recv_l, send_m, recv_m, send_a, recv_a, send_b, recv_b, send_z, recv_z,
 ):
     g = lax.axis_index("grp")
     d = lax.axis_index("dev")
     total = grps * devs
+    xs = devs // ZS
+    x = d // ZS
     me = g * devs + d
     above = lax.rem(me + 1, total)
     below = lax.rem(me + total - 1, total)
@@ -64,10 +68,16 @@
     def greet(pos):
         pl.semaphore_signal(barrier, inc=1, device_id=pos, device_id_type=MESH)
 
+    z = lax.rem(d, ZS)
+    first = d - z
+    z_up = (g, first + lax.rem(z + 1, ZS))
+    z_down = (g, first + lax.rem(z + ZS - 1, ZS))
     greet(at(above))
     greet(at(below))
+    greet(z_up)
+    greet(z_down)
     lax.fori_loop(1, grps, lambda i, c: (greet((lax.rem(g + i, grps), d)), c)[1], 0)
-    lax.fori_loop(1, devs, lambda i, c: (greet((g, lax.rem(d + i, devs))), c)[1], 0)
+    lax.fori_loop(1, xs, lambda i, c: (greet((g, lax.rem(d + ZS * i, devs))), c)[1], 0)
 
     for r in (leaf_t, par_t, gra_t, m_ref, a_ref, s_ref, acc_ref, tsum_ref):
         r[...] = jnp.zeros_like(r)
@@ -99,7 +109,7 @@
             src_ref=src, dst_ref=dst, send_sem=ss, recv_sem=rs, device_id=pos, device_id_type=MESH
         )
 
-    pl.semaphore_wait(barrier, 2 + grps - 1 + devs - 1)
+    pl.semaphore_wait(barrier, 4 + grps - 1 + xs - 1)
     leaf_up = copy(mine.at[1], got.at[0], send_l.at[0], recv_l.at[0], at(above))
     leaf_dn = copy(mine.at[0], got.at[1], send_l.at[1], recv_l.at[1], at(below))
     leaf_up.start()
@@ -135,11 +145,21 @@
     mid_dn.start()
 
     nclass = leaf_lists.shape[0]
+    for r in lists_in:
+        r.wait()
+    ml_ref[0:64, 0:nclass] = par_l[...]
+    ml_ref[64:72, 0:nclass] = gra_l[...]
+    mt_ref[0:128, :] = ml_ref[:, 0:128].T
+    mt_ref[128:256, :] = ml_ref[:, 128:256].T
+    for q in range(98):
+        s_ref[pl.ds(q, 8, stride=ROWS), 0:98] = sp[q].astype(F32)
     leaf_up.wait()
     leaf_dn.wait()
     w4[...] = jnp.concatenate(
         [b.astype(F32)[0:ROWS] for b in (got[0], mine[0], mine[1], got[1])], axis=0
     ).astype(BF)
+    for h, b in enumerate((got.at[0], mine.at[0], mine.at[1], got.at[1])):
+        win[:, 256 * h : 256 * h + 256] = b[...]
     mid_up.wait()
     mid_dn.wait()
     at = lax.broadcasted_iota(jnp.int16, (16, 128), 1)
@@ -164,15 +184,6 @@
                 take_lanes(high, (at + jnp.int16(52)) & jnp.int16(127)),
             ),
         )
-    for r in lists_in:
-        r.wait()
-    ml_ref[0:64, 0:nclass] = par_l[...]
-    ml_ref[64:72, 0:nclass] = gra_l[...]
-    mt_ref[0:128, :] = ml_ref[:, 0:128].T
-    mt_ref[128:256, :] = ml_ref[:, 128:256].T
-    for q in range(98):
-        s_ref[pl.ds(q, 8, stride=ROWS), 0:98] = sp[q].astype(F32)
-
     tr_in.wait()
     sub = lax.broadcasted_iota(jnp.int32, (8, 128), 0)
 
@@ -183,14 +194,46 @@
         w.wait_recv()
         return jnp.where(sub == frm, buf_a[frm], c)
 
-    msg_b[...] = lax.fori_loop(1, grps, wait_top, msg[...])
-
-    def send_block(i, c):
-        to = lax.rem(d + i, devs)
-        copy(msg_b, buf_b.at[d], send_b.at[i], recv_b.at[d], (g, to)).start()
+    mine_x = lax.fori_loop(1, grps, wait_top, msg[...])
+    msg_b[...] = mine_x
+
+    def send_x(i, c):
+        copy(msg_b, buf_b.at[x], send_b.at[i], recv_b.at[x], (g, lax.rem(d + ZS * i, devs))).start()
         return c
 
-    lax.fori_loop(1, devs, send_block, 0)
+    lax.fori_loop(1, xs, send_x, 0)
+
+    def wait_x(i, c):
+        to = lax.rem(d + ZS * i, devs)
+        frm = to // ZS
+        w = copy(msg_b, buf_b.at[frm], send_b.at[i], recv_b.at[frm], (g, to))
+        w.wait_send()
+        w.wait_recv()
+        ring[0, 0, frm] = buf_b[frm]
+        ring[1, 0, frm] = buf_b[frm]
+        return c
+
+    def hops(k):
+        return (
+            copy(ring.at[0, k], ring.at[0, k + 1], send_z.at[0, k], recv_z.at[0, k + 1], z_up),
+            copy(ring.at[1, k], ring.at[1, k + 1], send_z.at[1, k], recv_z.at[1, k + 1], z_down),
+        )
+
+    def hop(k):
+        @pl.when(k == 0)
+        def _():
+            ring[0, 0, x] = msg_b[...]
+            ring[1, 0, x] = msg_b[...]
+            lax.fori_loop(1, xs, wait_x, 0)
+
+        @pl.when(k > 0)
+        def _():
+            for c in hops(k - 1):
+                c.wait()
+
+        for c in hops(k):
+            c.start()
+
     sub = lax.broadcasted_iota(jnp.int16, (16, 512), 0)
     lane = lax.broadcasted_iota(jnp.int32, (16, 128), 1)
 
@@ -210,6 +253,20 @@
             hit = jnp.broadcast_to(hi == h, (ROWS, 512))
             picked = jnp.where(hit, r[h * ROWS : (h + 1) * ROWS], picked)
         g_ref[base : base + ROWS, 0:512] = picked.astype(BF)
+
+    def lanes_class(row, base):
+        for q in range(4):
+            cols = slice(128 * q, 128 * q + 128)
+            e = jnp.broadcast_to(row[:, cols], (16, 128))
+            lo = (e & 127).astype(jnp.int16)
+            hi = (e >> 7).astype(jnp.int16)
+            hits = [hi == jnp.int16(b) for b in range(8)]
+            for v in range(7):
+                rows = slice(16 * v, 16 * v + 16)
+                p = jnp.zeros((16, 128), BF)
+                for b in range(8):
+                    p = jnp.where(hits[b], take_lanes(win[rows, 128 * b : 128 * b + 128], lo), p)
+                g_ref[base + 16 * v : base + 16 * v + 16, cols] = p
 
     def mid_class(row, base):
         e = jnp.broadcast_to(row, (16, 128))
@@ -229,7 +286,8 @@
         lists = [leaf_lists[pl.ds(k0 + s, min(8, n - s)), :] for s in range(0, n, 8)]
         mids = [mt_ref[pl.ds(k0 + s, min(8, n - s)), :] for s in range(0, n, 8)]
         for c in range(n):
-            leaf_class(lists[c // 8][c % 8 : c % 8 + 1], c * 128)
+            pick = lanes_class if c in LANES else leaf_class
+            pick(lists[c // 8][c % 8 : c % 8 + 1], c * 128)
             mid_class(mids[c // 8][c % 8 : c % 8 + 1], c * 128)
         for s in range(0, n, 8):
             m = min(8, n - s)
@@ -243,24 +301,24 @@
     full = nclass // 16
 
     def step(j, carry):
+        @pl.when((lax.rem(j, 2) == 1) & (j < ZS))
+        def _():
+            hop(j // 2)
+
         group(pl.multiple_of(j * 16, 16), 16)
         return carry
 
     lax.fori_loop(0, full, step, 0)
     group(full * 16, nclass - full * 16)
 
-    def wait_block(i, c):
-        frm = lax.rem(d + i, devs)
-        w = copy(msg_b, buf_b.at[frm], send_b.at[i], recv_b.at[frm], (g, frm))
-        w.wait_send()
-        w.wait_recv()
-        tops[frm] = buf_b[frm]
-        return c
-
-    tops[d] = msg_b[...]
-    lax.fori_loop(1, devs, wait_block, 0)
+    for c in hops(ZS // 2 - 1):
+        c.wait()
+    for k in range(ZS // 2 + 1):
+        tops[lax.rem(z + ZS - k, ZS)] = ring[0, k]
+    for k in range(1, ZS // 2):
+        tops[lax.rem(z + k, ZS)] = ring[1, k]
     t = top_l[...]
-    t = jnp.broadcast_to(jnp.where(t >= 0, (t & 31) * 8 + (t >> 5), -1), (256, nclass))
+    t = jnp.broadcast_to(jnp.where(t >= 0, (t & 7) * 32 + (t & 24) + (t >> 5), -1), (256, nclass))
     hits = jnp.where(lax.broadcasted_iota(jnp.int32, (256, nclass), 0) == t, 1.0, 0.0).astype(BF)
     table = tops[...].reshape(256, 128).astype(BF)
     named = lax.dot_general(hits, table, (((0,), (0,)), ((), ())), preferred_element_type=F32)[:, 0:98]
@@ -323,9 +381,11 @@
                 vm((8, 128), F32),
                 vm((grps, 8, 128), F32),
                 vm((8, 128), F32),
-                vm((devs, 8, 128), F32),
-                vm((devs, 8, 128), F32),
+                vm((devs // ZS, 8, 128), F32),
+                vm((2, ZS // 2 + 1, devs // ZS, 8, 128), F32),
+                vm((ZS, devs // ZS, grps, 128), F32),
                 vm((4 * ROWS, 256), BF),
+                vm((112, 1024), BF),
                 vm((112, 128), BF),
                 vm((112, 128), BF),
                 vm((16 * 128, 640), BF),
@@ -337,10 +397,11 @@
                 vm((ROWS, 128), F32),
                 dma((10,)),
                 dma((2,)), dma((2,)), dma((2,)), dma((2,)),
-                dma((grps,)), dma((grps,)), dma((devs,)), dma((devs,)),
+                dma((grps,)), dma((grps,)), dma((devs // ZS,)), dma((devs // ZS,)),
+                dma((2, ZS // 2 + 1)), dma((2, ZS // 2 + 1)),
             ],
             compiler_params=pltpu.CompilerParams(
-                collective_id=0, has_side_effects=True, vmem_limit_bytes=48 << 20
+                collective_id=0, has_side_effects=True, vmem_limit_bytes=60 << 20
             ),
             name="fmm",
         )(*args)

time: 63 us -> 47.3 us (0.75)
  local copies, waits for them, and re-layouts: 10.6 us -> 1.63 us
  Pallas kernels: 52 us -> 45.6 us
    unnamed x21 -> x1, local copies, waits for them, and re-layouts: 10.6 us -> 1.63 us
    pallas_call x1, Pallas kernels: 52 us -> 45.6 us  [per_device(): pl.pallas_call(lambda *refs: kernel(grps, devs, *refs), out_shape=jax.Sha...]
where the time goes in v3:
time: 47.3 us; the launch traced here: 47.2 us
  Pallas kernels  45.6 us (96%)
  local copies, waits for them, and re-layouts  1.63 us (3%)
    pallas_call x1, Pallas kernels, per_device(): pl.pallas_call(lambda *refs: kernel(grps, devs, *refs), out_shape=jax.Sha...  45.6 us
    unnamed x1, local copies, waits for them, and re-layouts  1.63 us

profile of v3, /device:TPU:1, one launch (start us, length us, event | category | flops | bytes accessed | tf_op | source)
XLA Modules:
  0.0 47.2 jit_solution(4467483454787766507)
XLA Ops:
  0.0 45.6 %fmm.1 = f32[98,512]{1,0:T(8,128)} custom-call(bf16[512,256]{1,0:T(8,128)(2,1)} %refs_0_.1, s32[1,512]{1,0:T(1,128)} %bitcast.14, bf16[98,256]{1,0:T(8,128)(2,1)} %bitcast.12, bf16[98,8,98]{2,1,0:T(8,128)(2,1)} %bitcast.9, s32[189,512]{1,0:T(8,128)} %refs_4_.1, s32[64,189]{1,0:T(8,128)} %bitcast.11, s32[8,189]{1,0:T(8,128)} %bitcast.13, s32[1,189]{1,0:T(1,128)} %bitcast.15, ...), custom_call_target="tpu_custom_call" | custom-call | tf_op jit(solution)/shard_map/fmm/pallas_call | solution.py:366
  45.6 1.6 %copy.12 = f32[98,512]{1,0:T(8,128)} copy(f32[98,512]{1,0:T(8,128)} %fmm.1) | data formatting | bytes 401408

commit v4 on v3

--- a/solution.py
+++ b/solution.py
@@ -11,6 +11,7 @@
 MESH = pl.DeviceIdType.MESH
 ZS = 8
 LANES = (2, 6, 10, 14)
+EARLY = 4
 NT = (((1,), (1,)), ((), ()))
 
 
@@ -32,7 +33,7 @@
     strengths_h, counts_h, smap_h, mg_h, leaf_lists_h, par_h, gra_h, top_h, tr_h, sp_h, out,
     strengths, counts, smap, mg, leaf_lists, par_l, gra_l, top_l, tr, sp,
     m_ref, leaf_t, par_t, gra_t, mine, got, midm, midg, msg, buf_a, msg_b, buf_b, ring, tops,
-    w4, win, pwin, gwin, g_ref, a_ref, s_ref, ml_ref, mt_ref, acc_ref, tsum_ref,
+    w4, win, pwin, gwin, go_ref, g_ref, a_ref, s_ref, ml_ref, mt_ref, acc_ref, tsum_ref,
     load_sem, send_l, recv_l, send_m, recv_m, send_a, recv_a, send_b, recv_b, send_z, recv_z,
 ):
     g = lax.axis_index("grp")
@@ -153,13 +154,141 @@
     mt_ref[128:256, :] = ml_ref[:, 128:256].T
     for q in range(98):
         s_ref[pl.ds(q, 8, stride=ROWS), 0:98] = sp[q].astype(F32)
+    sub8 = lax.broadcasted_iota(jnp.int32, (8, 128), 0)
+
+    def wait_top(i, c):
+        frm = lax.rem(g + i, grps)
+        w = copy(msg, buf_a.at[frm], send_a.at[i], recv_a.at[frm], (frm, d))
+        w.wait_send()
+        w.wait_recv()
+        return jnp.where(sub8 == frm, buf_a[frm], c)
+
+    def send_x(i, c):
+        copy(msg_b, buf_b.at[x], send_b.at[i], recv_b.at[x], (g, lax.rem(d + ZS * i, devs))).start()
+        return c
+
+    def pass_x():
+        msg_b[...] = lax.fori_loop(1, grps, wait_top, msg[...])
+        lax.fori_loop(1, xs, send_x, 0)
+
+    def wait_x(i, c):
+        to = lax.rem(d + ZS * i, devs)
+        frm = to // ZS
+        w = copy(msg_b, buf_b.at[frm], send_b.at[i], recv_b.at[frm], (g, to))
+        w.wait_send()
+        w.wait_recv()
+        ring[0, 0, frm] = buf_b[frm]
+        ring[1, 0, frm] = buf_b[frm]
+        return c
+
+    def hops(k):
+        return (
+            copy(ring.at[0, k], ring.at[0, k + 1], send_z.at[0, k], recv_z.at[0, k + 1], z_up),
+            copy(ring.at[1, k], ring.at[1, k + 1], send_z.at[1, k], recv_z.at[1, k + 1], z_down),
+        )
+
+    def hop_first():
+        ring[0, 0, x] = msg_b[...]
+        ring[1, 0, x] = msg_b[...]
+        lax.fori_loop(1, xs, wait_x, 0)
+        for c in hops(0):
+            c.start()
+
+    def hop_next(k):
+        for c in hops(k - 1):
+            c.wait()
+        for c in hops(k):
+            c.start()
+
+    sub = lax.broadcasted_iota(jnp.int16, (16, 512), 0)
+    lane = lax.broadcasted_iota(jnp.int32, (16, 128), 1)
+
+    def place(slot, blocks, parts):
+        w4[slot * ROWS : (slot + 2) * ROWS, :] = jnp.concatenate(
+            [p[...].astype(F32)[0:ROWS] for p in parts], axis=0
+        ).astype(BF)
+        for h, p in zip(blocks, parts):
+            win[:, 256 * h : 256 * h + 256] = p[...]
+
+    def leaf_class(row, old, new, blocks):
+        lo = jnp.broadcast_to(row & 255, (16, 512)).astype(jnp.int16)
+        hi = row >> 8
+        onehot = jnp.concatenate(
+            [jnp.where(lo - jnp.int16(16 * i) == sub, BF(1), BF(0)) for i in range(16)], axis=0
+        )
+        at0 = 2 * ROWS if blocks[0] == 0 else 0
+        r = jnp.dot(w4[at0 : at0 + len(blocks) * ROWS, :], onehot, preferred_element_type=F32)
+        picked = jnp.zeros((ROWS, 512), F32) if old is None else old[0:ROWS, :].astype(F32)
+        for i, h in enumerate(blocks):
+            hit = jnp.broadcast_to(hi == h, (ROWS, 512))
+            picked = jnp.where(hit, r[i * ROWS : (i + 1) * ROWS], picked)
+        new[0:ROWS, 0:512] = picked.astype(BF)
+
+    def lanes_class(row, old, new, blocks):
+        for i in range(4):
+            cols = slice(128 * i, 128 * i + 128)
+            e = jnp.broadcast_to(row[:, cols], (16, 128))
+            lo = (e & 127).astype(jnp.int16)
+            hi = (e >> 7).astype(jnp.int16)
+            sources = [b for h in blocks for b in (2 * h, 2 * h + 1)]
+            hits = [hi == jnp.int16(b) for b in sources]
+            for v in range(7):
+                rows = slice(16 * v, 16 * v + 16)
+                p = jnp.zeros((16, 128), BF) if old is None else old[rows, cols]
+                for hit, b in zip(hits, sources):
+                    p = jnp.where(hit, take_lanes(win[rows, 128 * b : 128 * b + 128], lo), p)
+                new[rows, cols] = p
+
+    def mid_class(row, base):
+        e = jnp.broadcast_to(row, (16, 128))
+        lo = (e & 127).astype(jnp.int16)
+        is_p = ((lane < 64) & (e >= 0)).astype(jnp.int16) > 0
+        is_g = ((lane >= 64) & (lane < 72) & (e >= 0)).astype(jnp.int16) > 0
+        for v in range(7):
+            rows = slice(16 * v, 16 * v + 16)
+            x = jnp.zeros((16, 128), BF)
+            x = jnp.where(is_p, take_lanes(pwin[rows, :], lo), x)
+            x = jnp.where(is_g, take_lanes(gwin[rows, :], lo), x)
+            g_ref[base + 16 * v : base + 16 * v + 16, 512:640] = x
+
+    def lists_of(k0, n):
+        lists = [leaf_lists[pl.ds(k0 + i, min(8, n - i)), :] for i in range(0, n, 8)]
+        return [lists[c // 8][c % 8 : c % 8 + 1] for c in range(n)]
+
+    def pick(c, *rest):
+        (lanes_class if c in LANES else leaf_class)(*rest)
+
+    def own_group(j):
+        rows = lists_of(pl.multiple_of(j * 16, 16), 16)
+        for c in range(16):
+            pick(c, rows[c], None, go_ref.at[j, pl.ds(c * 128, 128), :], (1, 2))
+
+    def group(k0, n, early=None):
+        rows = lists_of(k0, n)
+        mids = [mt_ref[pl.ds(k0 + i, min(8, n - i)), :] for i in range(0, n, 8)]
+        for q in range(98):
+            a_ref[pl.ds(q, n, stride=ROWS), 0:98] = tr[q, pl.ds(k0, n), :].astype(F32)
+        for c in range(n):
+            new = g_ref.at[pl.ds(c * 128, 128), :]
+            if early is None:
+                pick(c, rows[c], None, new, (1, 2, 0, 3))
+            else:
+                pick(c, rows[c], go_ref.at[early, pl.ds(c * 128, 128), :], new, (0, 3))
+            mid_class(mids[c // 8][c % 8 : c % 8 + 1], c * 128)
+        for i in range(0, n, 8):
+            m = min(8, n - i)
+            ops = jnp.concatenate(
+                [a_ref[(i + c) * ROWS : (i + c + 1) * ROWS, :].astype(BF) for c in range(m)], axis=1
+            )
+            acc_ref[...] += jnp.dot(
+                ops, g_ref[i * 128 : (i + m) * 128, :], preferred_element_type=F32
+            )
+
+    place(0, (1, 2), (mine.at[0], mine.at[1]))
+    lax.fori_loop(0, EARLY, lambda j, c: (own_group(j), c)[1], 0)
     leaf_up.wait()
     leaf_dn.wait()
-    w4[...] = jnp.concatenate(
-        [b.astype(F32)[0:ROWS] for b in (got[0], mine[0], mine[1], got[1])], axis=0
-    ).astype(BF)
-    for h, b in enumerate((got.at[0], mine.at[0], mine.at[1], got.at[1])):
-        win[:, 256 * h : 256 * h + 256] = b[...]
+    place(2, (0, 3), (got.at[0], got.at[1]))
     mid_up.wait()
     mid_dn.wait()
     at = lax.broadcasted_iota(jnp.int16, (16, 128), 1)
@@ -185,132 +314,32 @@
             ),
         )
     tr_in.wait()
-    sub = lax.broadcasted_iota(jnp.int32, (8, 128), 0)
-
-    def wait_top(i, c):
-        frm = lax.rem(g + i, grps)
-        w = copy(msg, buf_a.at[frm], send_a.at[i], recv_a.at[frm], (frm, d))
-        w.wait_send()
-        w.wait_recv()
-        return jnp.where(sub == frm, buf_a[frm], c)
-
-    mine_x = lax.fori_loop(1, grps, wait_top, msg[...])
-    msg_b[...] = mine_x
-
-    def send_x(i, c):
-        copy(msg_b, buf_b.at[x], send_b.at[i], recv_b.at[x], (g, lax.rem(d + ZS * i, devs))).start()
-        return c
-
-    lax.fori_loop(1, xs, send_x, 0)
-
-    def wait_x(i, c):
-        to = lax.rem(d + ZS * i, devs)
-        frm = to // ZS
-        w = copy(msg_b, buf_b.at[frm], send_b.at[i], recv_b.at[frm], (g, to))
-        w.wait_send()
-        w.wait_recv()
-        ring[0, 0, frm] = buf_b[frm]
-        ring[1, 0, frm] = buf_b[frm]
-        return c
-
-    def hops(k):
-        return (
-            copy(ring.at[0, k], ring.at[0, k + 1], send_z.at[0, k], recv_z.at[0, k + 1], z_up),
-            copy(ring.at[1, k], ring.at[1, k + 1], send_z.at[1, k], recv_z.at[1, k + 1], z_down),
-        )
-
-    def hop(k):
-        @pl.when(k == 0)
+
+    def late_step(j, carry):
+        @pl.when(j == 0)
         def _():
-            ring[0, 0, x] = msg_b[...]
-            ring[1, 0, x] = msg_b[...]
-            lax.fori_loop(1, xs, wait_x, 0)
-
-        @pl.when(k > 0)
+            pass_x()
+
+        @pl.when(j == 2)
         def _():
-            for c in hops(k - 1):
-                c.wait()
-
-        for c in hops(k):
-            c.start()
-
-    sub = lax.broadcasted_iota(jnp.int16, (16, 512), 0)
-    lane = lax.broadcasted_iota(jnp.int32, (16, 128), 1)
-
-    def leaf_class(row, base):
-        lo = jnp.broadcast_to(row & 255, (16, 512)).astype(jnp.int16)
-        hi = row >> 8
-        onehot = jnp.concatenate(
-            [
-                jnp.where(lo - jnp.int16(16 * g) == sub, BF(1), BF(0))
-                for g in range(16)
-            ],
-            axis=0,
-        )
-        r = jnp.dot(w4[...], onehot, preferred_element_type=F32)
-        picked = jnp.zeros((ROWS, 512), F32)
-        for h in range(4):
-            hit = jnp.broadcast_to(hi == h, (ROWS, 512))
-            picked = jnp.where(hit, r[h * ROWS : (h + 1) * ROWS], picked)
-        g_ref[base : base + ROWS, 0:512] = picked.astype(BF)
-
-    def lanes_class(row, base):
-        for q in range(4):
-            cols = slice(128 * q, 128 * q + 128)
-            e = jnp.broadcast_to(row[:, cols], (16, 128))
-            lo = (e & 127).astype(jnp.int16)
-            hi = (e >> 7).astype(jnp.int16)
-            hits = [hi == jnp.int16(b) for b in range(8)]
-            for v in range(7):
-                rows = slice(16 * v, 16 * v + 16)
-                p = jnp.zeros((16, 128), BF)
-                for b in range(8):
-                    p = jnp.where(hits[b], take_lanes(win[rows, 128 * b : 128 * b + 128], lo), p)
-                g_ref[base + 16 * v : base + 16 * v + 16, cols] = p
-
-    def mid_class(row, base):
-        e = jnp.broadcast_to(row, (16, 128))
-        lo = (e & 127).astype(jnp.int16)
-        is_p = ((lane < 64) & (e >= 0)).astype(jnp.int16) > 0
-        is_g = ((lane >= 64) & (lane < 72) & (e >= 0)).astype(jnp.int16) > 0
-        for v in range(7):
-            rows = slice(16 * v, 16 * v + 16)
-            x = jnp.zeros((16, 128), BF)
-            x = jnp.where(is_p, take_lanes(pwin[rows, :], lo), x)
-            x = jnp.where(is_g, take_lanes(gwin[rows, :], lo), x)
-            g_ref[base + 16 * v : base + 16 * v + 16, 512:640] = x
-
-    def group(k0, n):
-        for q in range(98):
-            a_ref[pl.ds(q, n, stride=ROWS), 0:98] = tr[q, pl.ds(k0, n), :].astype(F32)
-        lists = [leaf_lists[pl.ds(k0 + s, min(8, n - s)), :] for s in range(0, n, 8)]
-        mids = [mt_ref[pl.ds(k0 + s, min(8, n - s)), :] for s in range(0, n, 8)]
-        for c in range(n):
-            pick = lanes_class if c in LANES else leaf_class
-            pick(lists[c // 8][c % 8 : c % 8 + 1], c * 128)
-            mid_class(mids[c // 8][c % 8 : c % 8 + 1], c * 128)
-        for s in range(0, n, 8):
-            m = min(8, n - s)
-            ops = jnp.concatenate(
-                [a_ref[(s + c) * ROWS : (s + c + 1) * ROWS, :].astype(BF) for c in range(m)], axis=1
-            )
-            acc_ref[...] += jnp.dot(
-                ops, g_ref[s * 128 : (s + m) * 128, :], preferred_element_type=F32
-            )
-
-    full = nclass // 16
+            hop_first()
+
+        group(pl.multiple_of(j * 16, 16), 16, j)
+        return carry
 
     def step(j, carry):
-        @pl.when((lax.rem(j, 2) == 1) & (j < ZS))
+        k = (j - EARLY + 2) // 2
+
+        @pl.when((lax.rem(j - EARLY, 2) == 0) & (k < ZS // 2))
         def _():
-            hop(j // 2)
+            hop_next(k)
 
         group(pl.multiple_of(j * 16, 16), 16)
         return carry
 
-    lax.fori_loop(0, full, step, 0)
-    group(full * 16, nclass - full * 16)
-
+    full = nclass // 16
+    lax.fori_loop(0, EARLY, late_step, 0)
+    lax.fori_loop(EARLY, full, step, 0)
     for c in hops(ZS // 2 - 1):
         c.wait()
     for k in range(ZS // 2 + 1):
@@ -325,6 +354,7 @@
     for q in range(98):
         tsum_ref[q : q + 1, 0:98] = jnp.sum(tr[q].astype(F32) * named, axis=0, keepdims=True)
     top = jnp.broadcast_to(0.125 * jnp.sum(tsum_ref[...], axis=1, keepdims=True), (ROWS, 128))
+    group(full * 16, nclass - full * 16)
 
     spread = s_ref[...].astype(BF)
     lane = lax.broadcasted_iota(jnp.int32, (ROWS, 128), 1)
@@ -388,6 +418,7 @@
                 vm((112, 1024), BF),
                 vm((112, 128), BF),
                 vm((112, 128), BF),
+                vm((EARLY, 16 * 128, 512), BF),
                 vm((16 * 128, 640), BF),
                 vm((16 * ROWS, 128), F32),
                 vm((8 * ROWS, 128), F32),

time: 47.3 us -> 45.2 us (0.956)
  Pallas kernels: 45.6 us -> 43.5 us
    pallas_call x1, Pallas kernels: 45.6 us -> 43.5 us  [per_device(): pl.pallas_call(lambda *refs: kernel(grps, devs, *refs), out_shape=jax.Sha...]
where the time goes in v4:
time: 45.2 us; the launch traced here: 45.1 us
  Pallas kernels  43.5 us (96%)
  local copies, waits for them, and re-layouts  1.63 us (4%)
    pallas_call x1, Pallas kernels, per_device(): pl.pallas_call(lambda *refs: kernel(grps, devs, *refs), out_shape=jax.Sha...  43.5 us
    unnamed x1, local copies, waits for them, and re-layouts  1.63 us

profile of v4, /device:TPU:1, one launch (start us, length us, event | category | flops | bytes accessed | tf_op | source)
XLA Modules:
  0.0 45.1 jit_solution(3867021560916646203)
XLA Ops:
  0.0 43.5 %fmm.1 = f32[98,512]{1,0:T(8,128)} custom-call(bf16[512,256]{1,0:T(8,128)(2,1)} %refs_0_.1, s32[1,512]{1,0:T(1,128)} %bitcast.14, bf16[98,256]{1,0:T(8,128)(2,1)} %bitcast.12, bf16[98,8,98]{2,1,0:T(8,128)(2,1)} %bitcast.9, s32[189,512]{1,0:T(8,128)} %refs_4_.1, s32[64,189]{1,0:T(8,128)} %bitcast.11, s32[8,189]{1,0:T(8,128)} %bitcast.13, s32[1,189]{1,0:T(1,128)} %bitcast.15, ...), custom_call_target="tpu_custom_call" | custom-call | tf_op jit(solution)/shard_map/fmm/pallas_call | solution.py:396
  43.5 1.6 %copy.12 = f32[98,512]{1,0:T(8,128)} copy(f32[98,512]{1,0:T(8,128)} %fmm.1) | data formatting | bytes 401408

commit v5 on v4

--- a/solution.py
+++ b/solution.py
@@ -11,7 +11,7 @@
 MESH = pl.DeviceIdType.MESH
 ZS = 8
 LANES = (2, 6, 10, 14)
-EARLY = 4
+EARLY = 7
 NT = (((1,), (1,)), ((), ()))
 
 
@@ -110,96 +110,6 @@
             src_ref=src, dst_ref=dst, send_sem=ss, recv_sem=rs, device_id=pos, device_id_type=MESH
         )
 
-    pl.semaphore_wait(barrier, 4 + grps - 1 + xs - 1)
-    leaf_up = copy(mine.at[1], got.at[0], send_l.at[0], recv_l.at[0], at(above))
-    leaf_dn = copy(mine.at[0], got.at[1], send_l.at[1], recv_l.at[1], at(below))
-    leaf_up.start()
-    leaf_dn.start()
-
-    mg_in.wait()
-    for q in range(98):
-        m_ref[pl.ds(q, 8, stride=ROWS), 0:98] = mg[q].astype(F32)
-    merge = jnp.concatenate([m_ref[ROWS * c : ROWS * c + ROWS, :].astype(BF) for c in range(8)], axis=1)
-
-    def merged(kids):
-        x = jnp.concatenate([k.astype(BF) for k in kids], axis=1)
-        y = lax.dot_general(x, merge, NT, preferred_element_type=F32)
-        return y.astype(BF).astype(F32)
-
-    par_t[:, 0:ROWS] = merged([leaf_t[pl.ds(c, 64, stride=8), :] for c in range(8)])
-    gra_t[:, 0:ROWS] = merged([par_t[pl.ds(c, 8, stride=8), :] for c in range(8)])
-    msg[...] = jnp.zeros_like(msg)
-    msg[:, 0:ROWS] = merged([jnp.broadcast_to(gra_t[c : c + 1, :], (8, 128)) for c in range(8)])
-
-    def send_top(i, c):
-        to = lax.rem(g + i, grps)
-        copy(msg, buf_a.at[g], send_a.at[i], recv_a.at[g], (to, d)).start()
-        return c
-
-    lax.fori_loop(1, grps, send_top, 0)
-
-    both = jnp.concatenate([par_t[...], gra_t[...], jnp.zeros((56, 128), F32)], axis=0)
-    midm[...] = both.T[0:112].astype(BF)
-    mid_up = copy(midm, midg.at[0], send_m.at[0], recv_m.at[0], at(above))
-    mid_dn = copy(midm, midg.at[1], send_m.at[1], recv_m.at[1], at(below))
-    mid_up.start()
-    mid_dn.start()
-
-    nclass = leaf_lists.shape[0]
-    for r in lists_in:
-        r.wait()
-    ml_ref[0:64, 0:nclass] = par_l[...]
-    ml_ref[64:72, 0:nclass] = gra_l[...]
-    mt_ref[0:128, :] = ml_ref[:, 0:128].T
-    mt_ref[128:256, :] = ml_ref[:, 128:256].T
-    for q in range(98):
-        s_ref[pl.ds(q, 8, stride=ROWS), 0:98] = sp[q].astype(F32)
-    sub8 = lax.broadcasted_iota(jnp.int32, (8, 128), 0)
-
-    def wait_top(i, c):
-        frm = lax.rem(g + i, grps)
-        w = copy(msg, buf_a.at[frm], send_a.at[i], recv_a.at[frm], (frm, d))
-        w.wait_send()
-        w.wait_recv()
-        return jnp.where(sub8 == frm, buf_a[frm], c)
-
-    def send_x(i, c):
-        copy(msg_b, buf_b.at[x], send_b.at[i], recv_b.at[x], (g, lax.rem(d + ZS * i, devs))).start()
-        return c
-
-    def pass_x():
-        msg_b[...] = lax.fori_loop(1, grps, wait_top, msg[...])
-        lax.fori_loop(1, xs, send_x, 0)
-
-    def wait_x(i, c):
-        to = lax.rem(d + ZS * i, devs)
-        frm = to // ZS
-        w = copy(msg_b, buf_b.at[frm], send_b.at[i], recv_b.at[frm], (g, to))
-        w.wait_send()
-        w.wait_recv()
-        ring[0, 0, frm] = buf_b[frm]
-        ring[1, 0, frm] = buf_b[frm]
-        return c
-
-    def hops(k):
-        return (
-            copy(ring.at[0, k], ring.at[0, k + 1], send_z.at[0, k], recv_z.at[0, k + 1], z_up),
-            copy(ring.at[1, k], ring.at[1, k + 1], send_z.at[1, k], recv_z.at[1, k + 1], z_down),
-        )
-
-    def hop_first():
-        ring[0, 0, x] = msg_b[...]
-        ring[1, 0, x] = msg_b[...]
-        lax.fori_loop(1, xs, wait_x, 0)
-        for c in hops(0):
-            c.start()
-
-    def hop_next(k):
-        for c in hops(k - 1):
-            c.wait()
-        for c in hops(k):
-            c.start()
-
     sub = lax.broadcasted_iota(jnp.int16, (16, 512), 0)
     lane = lax.broadcasted_iota(jnp.int32, (16, 128), 1)
 
@@ -239,6 +149,112 @@
                     p = jnp.where(hit, take_lanes(win[rows, 128 * b : 128 * b + 128], lo), p)
                 new[rows, cols] = p
 
+    def lists_of(k0, n):
+        lists = [leaf_lists[pl.ds(k0 + i, min(8, n - i)), :] for i in range(0, n, 8)]
+        return [lists[c // 8][c % 8 : c % 8 + 1] for c in range(n)]
+
+    def pick(c, *rest):
+        (lanes_class if c in LANES else leaf_class)(*rest)
+
+    def own_group(j):
+        rows = lists_of(pl.multiple_of(j * 16, 16), 16)
+        for c in range(16):
+            pick(c, rows[c], None, go_ref.at[j, pl.ds(c * 128, 128), :], (1, 2))
+
+    place(0, (1, 2), (mine.at[0], mine.at[1]))
+    lists_in[0].wait()
+    ahead = jnp.where(z == 0, 4, jnp.where(z == 1, 2, 0))
+    lax.fori_loop(0, ahead, lambda j, c: (own_group(j), c)[1], 0)
+    pl.semaphore_wait(barrier, 4 + grps - 1 + xs - 1)
+    leaf_up = copy(mine.at[1], got.at[0], send_l.at[0], recv_l.at[0], at(above))
+    leaf_dn = copy(mine.at[0], got.at[1], send_l.at[1], recv_l.at[1], at(below))
+    leaf_up.start()
+    leaf_dn.start()
+
+    mg_in.wait()
+    for q in range(98):
+        m_ref[pl.ds(q, 8, stride=ROWS), 0:98] = mg[q].astype(F32)
+    merge = jnp.concatenate([m_ref[ROWS * c : ROWS * c + ROWS, :].astype(BF) for c in range(8)], axis=1)
+
+    def merged(kids):
+        x = jnp.concatenate([k.astype(BF) for k in kids], axis=1)
+        y = lax.dot_general(x, merge, NT, preferred_element_type=F32)
+        return y.astype(BF).astype(F32)
+
+    par_t[:, 0:ROWS] = merged([leaf_t[pl.ds(c, 64, stride=8), :] for c in range(8)])
+    gra_t[:, 0:ROWS] = merged([par_t[pl.ds(c, 8, stride=8), :] for c in range(8)])
+    msg[...] = jnp.zeros_like(msg)
+    msg[:, 0:ROWS] = merged([jnp.broadcast_to(gra_t[c : c + 1, :], (8, 128)) for c in range(8)])
+
+    def send_top(i, c):
+        to = lax.rem(g + i, grps)
+        copy(msg, buf_a.at[g], send_a.at[i], recv_a.at[g], (to, d)).start()
+        return c
+
+    lax.fori_loop(1, grps, send_top, 0)
+
+    both = jnp.concatenate([par_t[...], gra_t[...], jnp.zeros((56, 128), F32)], axis=0)
+    midm[...] = both.T[0:112].astype(BF)
+    mid_up = copy(midm, midg.at[0], send_m.at[0], recv_m.at[0], at(above))
+    mid_dn = copy(midm, midg.at[1], send_m.at[1], recv_m.at[1], at(below))
+    mid_up.start()
+    mid_dn.start()
+
+    nclass = leaf_lists.shape[0]
+    for r in lists_in[1:]:
+        r.wait()
+    ml_ref[0:64, 0:nclass] = par_l[...]
+    ml_ref[64:72, 0:nclass] = gra_l[...]
+    mt_ref[0:128, :] = ml_ref[:, 0:128].T
+    mt_ref[128:256, :] = ml_ref[:, 128:256].T
+    for q in range(98):
+        s_ref[pl.ds(q, 8, stride=ROWS), 0:98] = sp[q].astype(F32)
+    sub8 = lax.broadcasted_iota(jnp.int32, (8, 128), 0)
+
+    def wait_top(i, c):
+        frm = lax.rem(g + i, grps)
+        w = copy(msg, buf_a.at[frm], send_a.at[i], recv_a.at[frm], (frm, d))
+        w.wait_send()
+        w.wait_recv()
+        return jnp.where(sub8 == frm, buf_a[frm], c)
+
+    def send_x(i, c):
+        copy(msg_b, buf_b.at[x], send_b.at[i], recv_b.at[x], (g, lax.rem(d + ZS * i, devs))).start()
+        return c
+
+    def pass_x():
+        msg_b[...] = lax.fori_loop(1, grps, wait_top, msg[...])
+        lax.fori_loop(1, xs, send_x, 0)
+
+    def wait_x(i, c):
+        to = lax.rem(d + ZS * i, devs)
+        frm = to // ZS
+        w = copy(msg_b, buf_b.at[frm], send_b.at[i], recv_b.at[frm], (g, to))
+        w.wait_send()
+        w.wait_recv()
+        ring[0, 0, frm] = buf_b[frm]
+        ring[1, 0, frm] = buf_b[frm]
+        return c
+
+    def hops(k):
+        return (
+            copy(ring.at[0, k], ring.at[0, k + 1], send_z.at[0, k], recv_z.at[0, k + 1], z_up),
+            copy(ring.at[1, k], ring.at[1, k + 1], send_z.at[1, k], recv_z.at[1, k + 1], z_down),
+        )
+
+    def hop_first():
+        ring[0, 0, x] = msg_b[...]
+        ring[1, 0, x] = msg_b[...]
+        lax.fori_loop(1, xs, wait_x, 0)
+        for c in hops(0):
+            c.start()
+
+    def hop_next(k):
+        for c in hops(k - 1):
+            c.wait()
+        for c in hops(k):
+            c.start()
+
     def mid_class(row, base):
         e = jnp.broadcast_to(row, (16, 128))
         lo = (e & 127).astype(jnp.int16)
@@ -250,18 +266,6 @@
             x = jnp.where(is_p, take_lanes(pwin[rows, :], lo), x)
             x = jnp.where(is_g, take_lanes(gwin[rows, :], lo), x)
             g_ref[base + 16 * v : base + 16 * v + 16, 512:640] = x
-
-    def lists_of(k0, n):
-        lists = [leaf_lists[pl.ds(k0 + i, min(8, n - i)), :] for i in range(0, n, 8)]
-        return [lists[c // 8][c % 8 : c % 8 + 1] for c in range(n)]
-
-    def pick(c, *rest):
-        (lanes_class if c in LANES else leaf_class)(*rest)
-
-    def own_group(j):
-        rows = lists_of(pl.multiple_of(j * 16, 16), 16)
-        for c in range(16):
-            pick(c, rows[c], None, go_ref.at[j, pl.ds(c * 128, 128), :], (1, 2))
 
     def group(k0, n, early=None):
         rows = lists_of(k0, n)
@@ -284,8 +288,7 @@
                 ops, g_ref[i * 128 : (i + m) * 128, :], preferred_element_type=F32
             )
 
-    place(0, (1, 2), (mine.at[0], mine.at[1]))
-    lax.fori_loop(0, EARLY, lambda j, c: (own_group(j), c)[1], 0)
+    lax.fori_loop(ahead, EARLY, lambda j, c: (own_group(j), c)[1], 0)
     leaf_up.wait()
     leaf_dn.wait()
     place(2, (0, 3), (got.at[0], got.at[1]))
@@ -324,15 +327,17 @@
         def _():
             hop_first()
 
+        @pl.when((lax.rem(j, 2) == 0) & (j >= 4) & (j < ZS + 2))
+        def _():
+            hop_next((j - 2) // 2)
+
         group(pl.multiple_of(j * 16, 16), 16, j)
         return carry
 
     def step(j, carry):
-        k = (j - EARLY + 2) // 2
-
-        @pl.when((lax.rem(j - EARLY, 2) == 0) & (k < ZS // 2))
+        @pl.when((lax.rem(j, 2) == 0) & (j < ZS + 2))
         def _():
-            hop_next(k)
+            hop_next((j - 2) // 2)
 
         group(pl.multiple_of(j * 16, 16), 16)
         return carry
@@ -348,35 +353,52 @@
         tops[lax.rem(z + k, ZS)] = ring[1, k]
     t = top_l[...]
     t = jnp.broadcast_to(jnp.where(t >= 0, (t & 7) * 32 + (t & 24) + (t >> 5), -1), (256, nclass))
-    hits = jnp.where(lax.broadcasted_iota(jnp.int32, (256, nclass), 0) == t, 1.0, 0.0).astype(BF)
+    named_at = jnp.where(lax.broadcasted_iota(jnp.int32, (256, nclass), 0) == t, 1.0, 0.0).astype(BF)
     table = tops[...].reshape(256, 128).astype(BF)
-    named = lax.dot_general(hits, table, (((0,), (0,)), ((), ())), preferred_element_type=F32)[:, 0:98]
+    named = lax.dot_general(named_at, table, (((0,), (0,)), ((), ())), preferred_element_type=F32)[:, 0:98]
+
+    def top_rows(first, last):
+        for q in range(first, last):
+            tsum_ref[q : q + 1, 0:98] = jnp.sum(tr[q].astype(F32) * named, axis=0, keepdims=True)
+
+    spread = s_ref[...].astype(BF)
+    lanes = lax.broadcasted_iota(jnp.int32, (ROWS, 128), 1)
+
+    def spread_from(v, index):
+        kids = (v if index is None else take_lanes(v, index)).astype(BF)
+        y = jnp.dot(
+            spread,
+            jnp.concatenate([kids, jnp.zeros((128 - ROWS, 128), BF)], axis=0),
+            preferred_element_type=F32,
+        )
+        r = y[0:ROWS]
+        for c in range(1, 8):
+            r = jnp.where((lanes & 7) == c, y[c * ROWS : (c + 1) * ROWS], r)
+        return r
+
+    k0 = full * 16
+    n = nclass - k0
+    rows = lists_of(k0, n)
+    mids = [mt_ref[k0 + i : k0 + min(i + 8, n), :] for i in range(0, n, 8)]
     for q in range(98):
-        tsum_ref[q : q + 1, 0:98] = jnp.sum(tr[q].astype(F32) * named, axis=0, keepdims=True)
-    top = jnp.broadcast_to(0.125 * jnp.sum(tsum_ref[...], axis=1, keepdims=True), (ROWS, 128))
-    group(full * 16, nclass - full * 16)
-
-    spread = s_ref[...].astype(BF)
-    lane = lax.broadcasted_iota(jnp.int32, (ROWS, 128), 1)
-
-    def spread_from(x, index):
-        picked = (x if index is None else take_lanes(x, index)).astype(BF)
-        z = jnp.dot(
-            spread,
-            jnp.concatenate([picked, jnp.zeros((128 - ROWS, 128), BF)], axis=0),
-            preferred_element_type=F32,
-        )
-        r = z[0:ROWS]
-        for c in range(1, 8):
-            r = jnp.where((lane & 7) == c, z[c * ROWS : (c + 1) * ROWS], r)
-        return r
-
-    mid = acc_ref[:, 512:640]
-    grand = 0.25 * mid + spread_from(top, None)
-    parent = 0.5 * mid + spread_from(grand, 64 + ((lane >> 3) & 7))
-    for g in range(4):
-        cols = slice(128 * g, 128 * g + 128)
-        out[:, cols] = (acc_ref[:, cols] + spread_from(parent, 16 * g + (lane >> 3)))[0:98]
+        a_ref[pl.ds(q, n, stride=ROWS), 0:98] = tr[q, k0:nclass, :].astype(F32)
+    ops = jnp.concatenate([a_ref[c * ROWS : (c + 1) * ROWS, :].astype(BF) for c in range(n)], axis=1)
+    for c in range(n):
+        mid_class(mids[c // 8][c % 8 : c % 8 + 1], c * 128)
+    mid = acc_ref[:, 512:640] + jnp.dot(ops, g_ref[0 : n * 128, 512:640], preferred_element_type=F32)
+    for c in range(n):
+        pick(c, rows[c], None, g_ref.at[c * 128 : (c + 1) * 128, :], (1, 2, 0, 3))
+        if c < 7:
+            top_rows(14 * c, 14 * c + 14)
+        if c == 7:
+            top = jnp.broadcast_to(0.125 * jnp.sum(tsum_ref[...], axis=1, keepdims=True), (ROWS, 128))
+            grand = 0.25 * mid + spread_from(top, None)
+        if c == 9:
+            parent = 0.5 * mid + spread_from(grand, 64 + ((lanes >> 3) & 7))
+    leaf = acc_ref[:, 0:512] + jnp.dot(ops, g_ref[0 : n * 128, 0:512], preferred_element_type=F32)
+    for i in range(4):
+        cols = slice(128 * i, 128 * i + 128)
+        out[:, cols] = (leaf[:, cols] + spread_from(parent, 16 * i + (lanes >> 3)))[0:98]
 
 
 def solution(mesh):
@@ -432,10 +454,10 @@
                 dma((2, ZS // 2 + 1)), dma((2, ZS // 2 + 1)),
             ],
             compiler_params=pltpu.CompilerParams(
-                collective_id=0, has_side_effects=True, vmem_limit_bytes=60 << 20
+                collective_id=0, has_side_effects=True, vmem_limit_bytes=48 << 20
             ),
             name="fmm",
-        )(*args)
+        )(*[pltpu.with_memory_space_constraint(a, pltpu.HBM) for a in args])
 
     rows = P(("grp", "dev"))
     cols = P(None, ("grp", "dev"))

time: 45.2 us -> 42.3 us (0.936)
  Pallas kernels: 43.5 us -> 41.5 us
  local copies, waits for them, and re-layouts: 1.63 us -> 0.69 us
    pallas_call x1, Pallas kernels: 43.5 us -> 41.5 us  [per_device(): pl.pallas_call(lambda *refs: kernel(grps, devs, *refs), out_shape=jax.Sha...]
    unnamed x1, local copies, waits for them, and re-layouts: 1.63 us -> 0.69 us
where the time goes in v5:
time: 42.3 us; the launch traced here: 42.2 us
  Pallas kernels  41.5 us (98%)
  local copies, waits for them, and re-layouts  0.69 us (2%)
    pallas_call x1, Pallas kernels, per_device(): pl.pallas_call(lambda *refs: kernel(grps, devs, *refs), out_shape=jax.Sha...  41.5 us

profile of v5, /device:TPU:1, one launch (start us, length us, event | category | flops | bytes accessed | tf_op | source)
XLA Modules:
  0.0 42.2 jit_solution(12653575796993003301)
XLA Ops:
  0.0 41.5 %fmm.1 = f32[98,512]{1,0:T(8,128)S(1)} custom-call(bf16[512,256]{1,0:T(8,128)(2,1)} %refs_0_.1, s32[1,512]{1,0:T(1,128)} %bitcast.14, bf16[98,256]{1,0:T(8,128)(2,1)} %bitcast.12, bf16[98,8,98]{2,1,0:T(8,128)(2,1)} %bitcast.9, s32[189,512]{1,0:T(8,128)} %refs_4_.1, s32[64,189]{1,0:T(8,128)} %bitcast.11, s32[8,189]{1,0:T(8,128)} %bitcast.13, ...), custom_call_target="tpu_custom_call" | custom-call | tf_op jit(solution)/shard_map/fmm/pallas_call | solution.py:418
  41.5 0.7 %copy.12 = f32[98,512]{1,0:T(8,128)} copy(f32[98,512]{1,0:T(8,128)S(1)} %fmm.1) | data formatting | bytes 401408

commit v6 on v5

--- a/solution.py
+++ b/solution.py
@@ -8,6 +8,7 @@
 BF = jnp.bfloat16
 F32 = jnp.float32
 ROWS = 104
+DEEP = 112
 MESH = pl.DeviceIdType.MESH
 ZS = 8
 LANES = (2, 6, 10, 14)
@@ -273,20 +274,16 @@
         for q in range(98):
             a_ref[pl.ds(q, n, stride=ROWS), 0:98] = tr[q, pl.ds(k0, n), :].astype(F32)
         for c in range(n):
-            new = g_ref.at[pl.ds(c * 128, 128), :]
+            new = g_ref.at[pl.ds(c * DEEP, DEEP), :]
             if early is None:
                 pick(c, rows[c], None, new, (1, 2, 0, 3))
             else:
                 pick(c, rows[c], go_ref.at[early, pl.ds(c * 128, 128), :], new, (0, 3))
-            mid_class(mids[c // 8][c % 8 : c % 8 + 1], c * 128)
-        for i in range(0, n, 8):
-            m = min(8, n - i)
-            ops = jnp.concatenate(
-                [a_ref[(i + c) * ROWS : (i + c + 1) * ROWS, :].astype(BF) for c in range(m)], axis=1
-            )
-            acc_ref[...] += jnp.dot(
-                ops, g_ref[i * 128 : (i + m) * 128, :], preferred_element_type=F32
-            )
+            mid_class(mids[c // 8][c % 8 : c % 8 + 1], c * DEEP)
+        ops = jnp.concatenate(
+            [a_ref[c * ROWS : (c + 1) * ROWS, 0:DEEP].astype(BF) for c in range(n)], axis=1
+        )
+        acc_ref[...] += jnp.dot(ops, g_ref[0 : n * DEEP, :], preferred_element_type=F32)
 
     lax.fori_loop(ahead, EARLY, lambda j, c: (own_group(j), c)[1], 0)
     leaf_up.wait()
@@ -382,12 +379,12 @@
     mids = [mt_ref[k0 + i : k0 + min(i + 8, n), :] for i in range(0, n, 8)]
     for q in range(98):
         a_ref[pl.ds(q, n, stride=ROWS), 0:98] = tr[q, k0:nclass, :].astype(F32)
-    ops = jnp.concatenate([a_ref[c * ROWS : (c + 1) * ROWS, :].astype(BF) for c in range(n)], axis=1)
+    ops = jnp.concatenate([a_ref[c * ROWS : (c + 1) * ROWS, 0:DEEP].astype(BF) for c in range(n)], axis=1)
     for c in range(n):
-        mid_class(mids[c // 8][c % 8 : c % 8 + 1], c * 128)
-    mid = acc_ref[:, 512:640] + jnp.dot(ops, g_ref[0 : n * 128, 512:640], preferred_element_type=F32)
+        mid_class(mids[c // 8][c % 8 : c % 8 + 1], c * DEEP)
+    mid = acc_ref[:, 512:640] + jnp.dot(ops, g_ref[0 : n * DEEP, 512:640], preferred_element_type=F32)
     for c in range(n):
-        pick(c, rows[c], None, g_ref.at[c * 128 : (c + 1) * 128, :], (1, 2, 0, 3))
+        pick(c, rows[c], None, g_ref.at[c * DEEP : (c + 1) * DEEP, :], (1, 2, 0, 3))
         if c < 7:
             top_rows(14 * c, 14 * c + 14)
         if c == 7:
@@ -395,7 +392,7 @@
             grand = 0.25 * mid + spread_from(top, None)
         if c == 9:
             parent = 0.5 * mid + spread_from(grand, 64 + ((lanes >> 3) & 7))
-    leaf = acc_ref[:, 0:512] + jnp.dot(ops, g_ref[0 : n * 128, 0:512], preferred_element_type=F32)
+    leaf = acc_ref[:, 0:512] + jnp.dot(ops, g_ref[0 : n * DEEP, 0:512], preferred_element_type=F32)
     for i in range(4):
         cols = slice(128 * i, 128 * i + 128)
         out[:, cols] = (leaf[:, cols] + spread_from(parent, 16 * i + (lanes >> 3)))[0:98]

time: 42.3 us -> 44.7 us (1.057)
  Pallas kernels: 41.5 us -> 43.9 us
    pallas_call x1, Pallas kernels: 41.5 us -> 43.9 us  [per_device(): pl.pallas_call(lambda *refs: kernel(grps, devs, *refs), out_shape=jax.Sha...]
where the time goes in v6:
time: 44.7 us; the launch traced here: 44.6 us
  Pallas kernels  43.9 us (98%)
  local copies, waits for them, and re-layouts  0.69 us (2%)
    pallas_call x1, Pallas kernels, per_device(): pl.pallas_call(lambda *refs: kernel(grps, devs, *refs), out_shape=jax.Sha...  43.9 us

profile of v6, /device:TPU:1, one launch (start us, length us, event | category | flops | bytes accessed | tf_op | source)
XLA Modules:
  0.0 44.6 jit_solution(11217696303675046373)
XLA Ops:
  0.0 43.9 %fmm.1 = f32[98,512]{1,0:T(8,128)S(1)} custom-call(bf16[512,256]{1,0:T(8,128)(2,1)} %refs_0_.1, s32[1,512]{1,0:T(1,128)} %bitcast.14, bf16[98,256]{1,0:T(8,128)(2,1)} %bitcast.12, bf16[98,8,98]{2,1,0:T(8,128)(2,1)} %bitcast.9, s32[189,512]{1,0:T(8,128)} %refs_4_.1, s32[64,189]{1,0:T(8,128)} %bitcast.11, s32[8,189]{1,0:T(8,128)} %bitcast.13, ...), custom_call_target="tpu_custom_call" | custom-call | tf_op jit(solution)/shard_map/fmm/pallas_call | solution.py:415
  43.9 0.7 %copy.12 = f32[98,512]{1,0:T(8,128)} copy(f32[98,512]{1,0:T(8,128)S(1)} %fmm.1) | data formatting | bytes 401408
